TPU v7x, 32 devices: a whole 2x2x4 slice. The times are simulated.
32 devices in a mesh: groups: 2 (over y), gx: 4 (over z), gy: 2 (over x), gz: 2 (over core).
Axes of the slice: x: 2, y: 2, z: 4, core: 2. Of those that a mesh axis runs over, the one named last changes fastest.
Arguments:
- prompt_rows: bfloat16 [1024, 8192], P(('groups', 'gx', 'gz'), 'gy'), parts along dimension 0, may hold values from -6 to 6
- gate_up: bfloat16 [8192, 2, 28672], P('gy', None, ('gx', 'gz')), may hold values from -0.0625 to 0.0625
- queries: bfloat16 [2, 128, 8192], P(None, ('groups', 'gy'), ('gx', 'gz')), parts along dimension 1, may hold values from -128 to 128
- new_kv: bfloat16 [2, 128, 1024], P(None, ('groups', 'gy')), parts along dimension 1, may hold values from -6 to 6
- kv_cache: bfloat16 [128, 2048, 1024], P(('groups', 'gy'), ('gx', 'gz')), parts along dimension 0, may hold values from -6 to 6
- lengths: int32 [128], P(('groups', 'gy')), parts along dimension 0, may hold values from 2 to 2048, as said below
Outputs:
- hidden_units: bfloat16 [1024, 28672], P(('groups', 'gy'), ('gx', 'gz')), parts along dimension 0
- attended: bfloat16 [2, 128, 8192], P(None, ('groups', 'gy'), ('gx', 'gz')), parts along dimension 1
There are 2 independent parts, one for each index of `groups`. A program takes and returns all parts, laid end to end along the dimension named above; an argument that names none is the same for every part. Nothing has to cross between parts.
Inputs may be any that keep to these rules, and one draw needn't show every extreme that they name: Slots 0 to lengths[b] - 1 of sequence b are live; some sequence has exactly 2048.
All inputs are finite; a program needn't handle non-finite values.
Results may differ from a plain program's by a relative error of at most 0.024.
Values may be sent and summed in bfloat16 or wider, within the bound.
No kernel may reach another device: no remote copies, remote signals or barrier semaphores. Data moves between devices by JAX's collectives and lax.ppermute only.
A program may use at most 256 MiB of HBM per device.

v0:
```python
import math

import jax
import jax.numpy as jnp
from jax import lax
from jax.sharding import PartitionSpec as P

KVH = 4
HD = 128


lowest = -1e30


def joined(x, axis, join):
    gathered = jax.tree.map(
        lambda a, kind: lax.all_gather(a.astype(kind), axis),
        x,
        (jnp.bfloat16, jnp.bfloat16, jnp.bfloat16),
    )

    def take(source):
        return jax.tree.map(
            lambda a, own: lax.dynamic_index_in_dim(a, source, 0, False).astype(own.dtype),
            gathered,
            x,
        )

    return lax.fori_loop(
        1, lax.axis_size(axis), lambda source, state: join(state, take(source)), take(0)
    )


def local_attention(grouped, cache_units, fresh_units, limits, offset, holds_new):
    step_count = grouped.shape[0]
    unit_count = cache_units.shape[0]
    positions_local = cache_units.shape[1]
    combined = jnp.concatenate([cache_units, jnp.transpose(fresh_units, (1, 0, 2, 3, 4))], axis=1)
    key_rows = combined[:, :, 0]
    value_rows = combined[:, :, 1]
    scores = jnp.einsum(
        "sukgd,ujkd->sukgj", grouped, key_rows, preferred_element_type=jnp.float32
    ) * (1.0 / math.sqrt(HD))
    absolute = offset + jnp.arange(positions_local, dtype=jnp.int32)
    cached = absolute[None, :] < limits[:, None]
    step_ids = jnp.arange(step_count, dtype=jnp.int32)
    new_visible = (step_ids[None, :] <= step_ids[:, None]) & holds_new
    visible = jnp.concatenate(
        [
            jnp.broadcast_to(cached[None], (step_count, unit_count, positions_local)),
            jnp.broadcast_to(new_visible[:, None, :], (step_count, unit_count, step_count)),
        ],
        axis=2,
    )
    visible_mask = visible[:, :, None, None, :]
    masked = jnp.where(visible_mask, scores, lowest)
    row_max = jnp.max(masked, axis=-1)
    probabilities = jnp.where(visible_mask, jnp.exp(masked - row_max[..., None]), 0.0)
    denominator = jnp.sum(probabilities, axis=-1)
    weights = probabilities.astype(jnp.bfloat16)
    numerator = jnp.einsum(
        "sukgj,ujkd->sukgd", weights, value_rows, preferred_element_type=jnp.float32
    )
    return (numerator, row_max, denominator)


def join_partials(earlier, later):
    overall = jnp.maximum(earlier[1], later[1])
    left_scale = jnp.exp(earlier[1] - overall)
    right_scale = jnp.exp(later[1] - overall)
    return (
        earlier[0] * left_scale[..., None] + later[0] * right_scale[..., None],
        overall,
        earlier[2] * left_scale + later[2] * right_scale,
    )


def on_device(prompt_rows, gate_up, queries, new_kv, kv_cache, lengths):
    flat_weights = gate_up.reshape(gate_up.shape[0], -1)
    partial_terms = jnp.dot(
        lax.all_gather(prompt_rows, ("gx", "gz"), axis=0, tiled=True),
        flat_weights,
        preferred_element_type=jnp.float32,
    )
    summed = lax.psum_scatter(
        partial_terms.astype(jnp.bfloat16), "gy", scatter_dimension=0, tiled=True
    ).astype(jnp.float32)
    summed = summed.reshape(summed.shape[0], 2, -1)
    hidden_units = (jax.nn.silu(summed[:, 0]) * summed[:, 1]).astype(jnp.bfloat16)
    members = lax.axis_size(("gx", "gz"))
    my_index = lax.axis_index(("gx", "gz"))
    step_count = queries.shape[0]
    sequences = kv_cache.shape[0]
    positions_local = kv_cache.shape[1]
    all_heads = lax.all_gather(queries, ("gx", "gz"), axis=2, tiled=True)
    groups_per = all_heads.shape[2] // (KVH * HD)
    grouped = all_heads.reshape(step_count, sequences, KVH, groups_per, HD)
    cache_units = kv_cache.reshape(sequences, positions_local, 2, KVH, HD)
    fresh_units = new_kv.reshape(step_count, sequences, 2, KVH, HD)
    numerator, row_max, denominator = local_attention(
        grouped, cache_units, fresh_units, lengths, my_index * positions_local, my_index == 0
    )
    numerator = numerator.reshape(step_count, sequences, -1, HD)
    row_max = row_max.reshape(step_count, sequences, -1)
    denominator = denominator.reshape(step_count, sequences, -1)
    per_dev = numerator.shape[2] // members
    numerator, row_max, denominator = joined(
        (numerator, row_max, denominator), ("gx", "gz"), join_partials
    )
    numerator = lax.dynamic_slice_in_dim(numerator, my_index * per_dev, per_dev, 2)
    denominator = lax.dynamic_slice_in_dim(denominator, my_index * per_dev, per_dev, 2)
    attended = (
        (numerator / denominator[..., None]).reshape(step_count, sequences, -1).astype(jnp.bfloat16)
    )
    return (hidden_units, attended)


def solution(mesh):
    return jax.shard_map(
        on_device,
        mesh=mesh,
        in_specs=(
            P(("groups", "gx", "gz"), "gy"),
            P("gy", None, ("gx", "gz")),
            P(None, ("groups", "gy"), ("gx", "gz")),
            P(None, ("groups", "gy"), None),
            P(("groups", "gy"), ("gx", "gz"), None),
            P(("groups", "gy")),
        ),
        out_specs=(P(("groups", "gy"), ("gx", "gz")), P(None, ("groups", "gy"), ("gx", "gz"))),
        check_vma=False,
    )
```

profile of v0, /device:TPU:0, one launch (start us, length us, event | category | flops | bytes accessed | tf_op | source)
XLA Modules:
  0.0 281.8 jit_solution(15507614478177896397)
XLA Ops:
  7.2 0.0 all-gather.6.cloned.1.call-start
  7.2 0.7 all-gather.6.cloned.1.call-update
  7.9 0.0 all-gather.4.cloned.1.call-start
  7.9 0.7 all-gather.4.cloned.1.call-update
  8.6 0.0 all-gather.8.cloned.1.call-start
  8.7 1.0 reshape.123
  9.7 0.1 copy.64
  9.8 22.5 %copy.36 = bf16[32,256,1024]{1,2,0:T(8,128)(2,1)} copy(bf16[32,256,1024]{2,1,0:T(8,128)(2,1)} %param.12) | data formatting | bytes 33554432 | tf_op args[4]
  32.3 21.4 %copy.38 = bf16[32,256,2,4,128]{4,1,3,0,2:T(8,128)(2,1)} copy(bf16[32,256,2,4,128]{1,4,3,2,0:T(8,128)(2,1)} %bitcast.93) | data formatting | bytes 33554432 | tf_op jit(solution)/shard_map/reshape | solution.py:98
  53.8 0.0 copy-done.1
  53.8 0.1 broadcast_compare_fusion
  53.9 0.1 pad_add_fusion
  54.0 0.0 all-gather.6.cloned.1.call-done
  54.0 1.5 copy.50
  55.5 6.1 %fusion.11 = (f32[2,32,4,16]{3,0,2,1:T(2,128)S(1)}, f32[32,4,258,2,16]{2,4,3,1,0:T(8,128)S(1)}) fusion(pred[2,32,258]{2,0,1:T(4,128)(4,1)S(1)} %pad_add_fusion, bf16[2,32,4,16,128]{4,3,2,1,0:T(8,128)(2,1)S(1)} %bitcast.97, bf16[32,2,2,4,128]{4,1,3,0,2:T(2,128)(2,1)S(1)} %bitcast.99, bf16[32,256,2,4,128]{4,1,3,0,2:T(8,128)(2,1)} %copy.38), kind=kOutput, calls=%fused_computation.20 | convolution fusion | flops 290607104 | bytes 22216832 | tf_op jit(solution)/shard_map/sukgd,ujkd->sukgj/dot_general | solution.py:41
  61.6 0.0 copy-start
  61.6 7.2 %fusion.27 = bf16[2,32,4,16,128]{4,3,0,2,1:T(8,128)(2,1)S(1)} fusion(f32[32,4,258,2,16]{2,4,3,1,0:T(8,128)S(1)} %get-tuple-element.209, f32[2,32,4,16]{3,0,2,1:T(2,128)S(1)} %get-tuple-element.208, pred[2,32,258]{2,0,1:T(4,128)(4,1)S(1)} %pad_add_fusion, bf16[32,256,2,4,128]{4,1,3,0,2:T(8,128)(2,1)} %copy.38, bf16[32,2,2,4,128]{4,1,3,0,2:T(2,128)(2,1)S(1)} %bitcast.100), kind=kOutput, calls=%fused_computation.33 | convolution fusion | flops 293249024 | bytes 22216832 | tf_op jit(solution)/shard_map/sukgj,ujkd->sukgd/dot_general | solution.py:61
  68.8 0.0 copy-done
  68.8 1.3 copy.40
  70.1 0.0 all-gather.8.cloned.1.call-update
  70.2 0.2 reduce-scatter.2.cloned.1.call-start
  70.4 40.3 %copy.49 = bf16[512,8,2,3584]{3,1,2,0:T(8,128)(2,1)} copy(bf16[512,8,2,3584]{3,2,1,0:T(2,128)(2,1)} %bitcast.94) | data formatting | bytes 117440512
  110.7 38.9 %convolution_convert_fusion = bf16[512,7168]{1,0:T(8,128)(2,1)} fusion(bf16[512,4096]{1,0:T(8,128)(2,1)} %all-gather.4.cloned.1.call-done, bf16[4096,7168]{1,0:T(8,128)(2,1)} %bitcast.95), kind=kOutput, calls=%fused_computation.10 | convolution fusion | flops 30068441088 | bytes 70254592 | tf_op jit(solution)/shard_map/dot_general | solution.py:80
  149.5 0.0 reduce-scatter.2.cloned.1.call-update
  149.5 0.1 copy.41
  149.6 0.1 copy.42
  149.7 4.4 %fusion.12 = bf16[2,32,4,16]{3,0,2,1:T(2,128)(2,1)S(1)} fusion(f32[32,4,258,2,16]{2,4,3,1,0:T(8,128)} %copy-done, f32[2,32,4,16]{3,0,2,1:T(2,128)S(1)} %get-tuple-element.208, pred[2,32,258]{2,0,1:T(4,128)(4,1)S(1)} %pad_add_fusion), kind=kLoop, calls=%fused_computation.21 | loop fusion | flops 5279744 | bytes 4268160 | tf_op jit(solution)/shard_map/reduce_sum | solution.py:59
  154.2 0.1 copy.43
  154.3 0.1 copy.44
  154.4 16.2 %all_gather.21 = bf16[8,2,32,64]{3,2,1,0:T(8,128)(2,1)S(1)} all-gather(bf16[1,2,32,64]{3,2,1,0:T(8,128)(2,1)S(1)} %copy.42), channel_id=1, replica_groups=mesh['groups'=2,'gx'=4,'gy'=2,'gz'=2] {'gx','gz'}, dimensions={0}, use_global_device_ids=true | all-gather | bytes 73728 | tf_op jit(solution)/shard_map/all_gather | solution.py:17
  170.6 14.2 %all_gather.22 = bf16[8,2,32,64]{3,2,1,0:T(8,128)(2,1)S(1)} all-gather(bf16[1,2,32,64]{3,2,1,0:T(8,128)(2,1)S(1)} %copy.44), channel_id=1, replica_groups=mesh['groups'=2,'gx'=4,'gy'=2,'gz'=2] {'gx','gz'}, dimensions={0}, use_global_device_ids=true | all-gather | bytes 73728 | tf_op jit(solution)/shard_map/all_gather | solution.py:17
  184.8 0.0 all-gather.8.cloned.1.call-done
  184.8 1.5 fusion.32
  186.3 18.3 %while.19 = (s32[]{:T(128)}, f32[2,32,64,128]{3,2,1,0:T(8,128)S(1)}, f32[2,32,64]{2,1,0:T(8,128)S(1)}, f32[2,32,64]{2,1,0:T(8,128)S(1)}, bf16[8,2,32,64]{3,2,1,0...) while((s32[]{:T(128)}, ...), condition=%wide.region_4.5_spmd, body=%wide.region_3.4_spmd.sunk | while | flops 2129925 | bytes 5390487 | solution.py:29
  186.3 2.6 fusion.48
  189.0 2.5 fusion.48
  191.6 2.5 fusion.48
  194.2 2.5 fusion.48
  196.8 2.5 fusion.48
  199.4 2.5 fusion.48
  202.0 2.5 fusion.48
  204.6 0.1 constant_dynamic-slice_fusion
  204.6 0.1 divide_convert_fusion
  204.8 0.7 convert_element_type.132
  205.5 49.8 %reduce-scatter.2.cloned.1.call-done = bf16[256,7168]{1,0:T(8,128)(2,1)} async-done(((bf16[512,7168]{1,0:T(8,128)(2,1)}), bf16[256,7168]{1,0:T(8,128)(2,1)}) %reduce-scatter.2.cloned.1.call-update) | async-done | bytes 3670032 | tf_op jit(solution)/shard_map/reduce_scatter | solution.py:85
  255.3 9.7 %reshape.129 = f32[256,2,3584]{2,1,0:T(2,128)} reshape(bf16[256,7168]{1,0:T(8,128)(2,1)} %reduce-scatter.2.cloned.1.call-done) | data formatting | bytes 11010048 | tf_op jit(solution)/shard_map/reshape | solution.py:88
  265.0 8.0 %fusion.42 = (f32[256,1,3584]{2,1,0:T(1,128)S(1)}, f32[256,1,3584]{2,1,0:T(1,128)S(1)}) fusion(f32[256,2,3584]{2,1,0:T(2,128)} %reshape.129), kind=kLoop, calls=%fused_computation.53 | loop fusion | bytes 14680064 | tf_op jit(solution)/shard_map/slice | solution.py:89
  273.0 2.3 fusion.15
  (15 shorter events, 0.3 us)
Async XLA Ops:
  7.2 46.8 %all-gather.6.cloned.1.call-start = ((), (), s32[]{:S(2)}) async-start(), calls=%async_computation.3 | async-start | bytes 1179648 | tf_op jit(solution)/shard_map/all_gather | solution.py:95
  7.9 102.8 %all-gather.4.cloned.1.call-start = ((), (), s32[]{:S(2)}) async-start(), calls=%async_computation.1 | async-start | bytes 4718592 | tf_op jit(solution)/shard_map/all_gather | solution.py:81
  8.6 176.1 %all-gather.8.cloned.1.call-start = ((), (), s32[]{:S(2)}) async-start(), calls=%async_computation.4 | async-start | bytes 9437184 | tf_op jit(solution)/shard_map/all_gather | solution.py:17
  32.3 21.4 %copy-start.1 = (s32[32]{0:T(128)S(1)}, s32[32]{0:T(128)}, u32[]{:S(2)}) copy-start(s32[32]{0:T(128)} %param.13) | copy-start | bytes 388
  61.6 7.2 %copy-start = (f32[32,4,258,2,16]{2,4,3,1,0:T(8,128)}, f32[32,4,258,2,16]{2,4,3,1,0:T(8,128)S(1)}, u32[]{:S(2)}) copy-start(f32[32,4,258,2,16]{2,4,3,1,0:T(8,128)S(1)} %get-tuple-element.209) | copy-start | bytes 12681220
  70.2 185.2 %reduce-scatter.2.cloned.1.call-start = ((), (), s32[]{:S(2)}) async-start(), calls=%async_computation.2 | async-start | bytes 11010048 | tf_op jit(solution)/shard_map/reduce_scatter | solution.py:85
Sparse Core Ops, SparseCore 0:
  9.6 24.7 all-gather.5
  36.0 46.7 all-gather.3
  85.0 81.2 all-gather.7
  168.5 86.7 reduce-scatter.1
where the time goes:
time: 283 us; the launch traced here: 282 us
  local copies, waits for them, and re-layouts  107 us (38%)
  matrix products  52.1 us (18%)
  waiting for transfers between devices  51.3 us (18%)
  blocking collectives  30.4 us (11%)
  other arithmetic  26.6 us (9%)
  between operations  13.9 us (5%)
    unnamed x7, local copies, waits for them, and re-layouts  64.3 us
    reduce_scatter x1, waiting for transfers between devices, on_device(): lax.psum_scatter(partial_terms.astype(jnp.bfloat16), 'gy', scatter_dimens...  49.8 us
    dot_general x1, matrix products, on_device(): jnp.dot(lax.all_gather(prompt_rows, ('gx', 'gz'), axis=0, tiled=True), fl...  38.9 us
    all_gather x2, blocking collectives, joined(): lax.all_gather(a.astype(kind), axis)  30.4 us
    reshape x1, local copies, waits for them, and re-layouts, on_device(): cache_units = kv_cache.reshape(sequences, positions_local, 2, KVH, HD)  21.4 us
    add x7, other arithmetic, join_partials(): earlier[0] * left_scale[..., None] + later[0] * right_scale[..., None]  17.8 us
    reshape x1, local copies, waits for them, and re-layouts, on_device(): summed = summed.reshape(summed.shape[0], 2, -1)  9.68 us
    slice x1, local copies, waits for them, and re-layouts, on_device(): summed[:, 0]  7.99 us
  transfers between devices with their start and end apart: 4, of which 1 were waited for; matrix products, arithmetic and copies ran while one was open for 59% of the time, Pallas kernels for 0%

commit v1 on v0

v1 whole, which is shorter than its diff:
```python
import functools
import math

import jax
import jax.numpy as jnp
from jax import lax
from jax.experimental import pallas as pl
from jax.experimental.pallas import tpu as pltpu
from jax.sharding import PartitionSpec as P

KVH = 4
HD = 128
lowest = -1e30
f32 = jnp.float32
bf16 = jnp.bfloat16
SHORT = pl.CostEstimate(flops=1, bytes_accessed=1, transcendentals=0)


def xor_pairs(axis, bit):
    return [(i, i ^ bit) for i in range(lax.axis_size(axis))]


def both_cores(x):
    other = lax.ppermute(x, "gz", [(0, 1), (1, 0)])
    first = lax.axis_index("gz") == 0
    return jnp.where(first, x, other), jnp.where(first, other, x)


def attention_kernel(limits_ref, *refs, per_step, members):
    q_ref, kv_ref, num_ref, stat_ref = refs[-4:]
    rows = q_ref.shape[2]
    slots = kv_ref.shape[1]
    half = kv_ref.shape[2] // 2
    total = members * rows
    share = members // KVH
    step = pl.program_id(0)
    slot = lax.broadcasted_iota(jnp.int32, (slots, total), 0)
    zero = jnp.zeros((rows * share, HD), bf16)
    for i in range(per_step):
        limit = limits_ref[step * per_step + i]
        wide = []
        for k in range(KVH):
            mine = jnp.concatenate([q_ref[k * share + m, i] for m in range(share)], axis=0)
            wide.append(jnp.concatenate([mine if j == k else zero for j in range(KVH)], axis=1))
        wide = jnp.concatenate(wide, axis=0)
        scores = lax.dot_general(
            kv_ref[i, :, :half], wide, (((1,), (1,)), ((), ())), preferred_element_type=f32
        ) * (1.0 / math.sqrt(HD))
        seen = slot < limit
        scores = jnp.where(seen, scores, lowest)
        top = jnp.max(scores, axis=0, keepdims=True)
        probs = jnp.where(seen, jnp.exp(scores - top), 0.0)
        stat_ref[0, i : i + 1, :] = top
        stat_ref[1, i : i + 1, :] = jnp.sum(probs, axis=0, keepdims=True)
        weights = probs.T.astype(bf16)
        full = jnp.dot(weights, kv_ref[i, :, half:], preferred_element_type=f32)
        for m in range(members):
            k = m // share
            num_ref[m, i] = full[m * rows : (m + 1) * rows, k * HD : (k + 1) * HD].astype(bf16)


def cached_attention(all_q, kv_cache, limits, *tokens):
    members, sequences, rows, _ = all_q.shape
    slots, width = kv_cache.shape[1:]
    per_step = 8
    total = members * rows
    return pl.pallas_call(
        functools.partial(attention_kernel, per_step=per_step, members=members),
        grid_spec=pltpu.PrefetchScalarGridSpec(
            num_scalar_prefetch=1,
            grid=(sequences // per_step,),
            in_specs=[pl.BlockSpec(memory_space=pl.ANY)] * len(tokens)
            + [
                pl.BlockSpec((members, per_step, rows, HD), lambda j, _: (0, j, 0, 0)),
                pl.BlockSpec((per_step, slots, width), lambda j, _: (j, 0, 0)),
            ],
            out_specs=[
                pl.BlockSpec((members, per_step, rows, HD), lambda j, _: (0, j, 0, 0)),
                pl.BlockSpec((2, per_step, total), lambda j, _: (0, j, 0)),
            ],
        ),
        out_shape=[
            jax.ShapeDtypeStruct((members, sequences, rows, HD), bf16),
            jax.ShapeDtypeStruct((2, sequences, total), f32),
        ],
        compiler_params=pltpu.CompilerParams(vmem_limit_bytes=40 << 20),
        cost_estimate=SHORT,
    )(limits, *tokens, all_q, kv_cache)


def lane_kernel(x_ref, out_ref):
    half = x_ref.shape[1] // 2
    row = lax.broadcasted_iota(jnp.int32, (256, 256), 0)
    col = lax.broadcasted_iota(jnp.int32, (256, 256), 1)
    place = (col == 2 * (row % 128) + row // 128).astype(f32).astype(bf16)
    for c in range(half // 128):
        both = jnp.concatenate(
            [x_ref[:, c * 128 : (c + 1) * 128], x_ref[:, half + c * 128 : half + (c + 1) * 128]],
            axis=1,
        )
        moved = jnp.dot(both, place, preferred_element_type=f32)
        out_ref[:, c * 256 : (c + 1) * 256] = moved.astype(bf16)


def interleave_lanes(x):
    return pl.pallas_call(
        lane_kernel,
        out_shape=jax.ShapeDtypeStruct(x.shape, bf16),
        cost_estimate=SHORT,
    )(x)


def split_rows(first, second):
    rows = first.shape[0]
    odd = (lax.broadcasted_iota(jnp.int32, (1, 8, 128), 1) & 1) == 1
    a = first.astype(f32).reshape(rows // 8, 8, 128)
    b = second.astype(f32).reshape(rows // 8, 8, 128)
    gate = jnp.where(odd, pltpu.roll(b, 1, 1), a)
    up = jnp.where(odd, b, pltpu.roll(a, 7, 1))
    return gate.reshape(rows, 128).astype(bf16), up.reshape(rows, 128).astype(bf16)


def product_kernel(*refs, count, cuts):
    x_ref, left_ref, right_ref = refs[-5 - len(cuts) : -2 - len(cuts)]
    outs, (flat, sems) = refs[-2 - len(cuts) : -2], refs[-2:]
    j = pl.program_id(0)
    depth = left_ref.shape[0]
    piece = min(1024, depth)
    halves = [r.reshape(2 * depth, 128) for r in (left_ref, right_ref)]

    def copies(slot):
        return [
            pltpu.make_async_copy(h, flat.at[slot, t], sems.at[slot, t])
            for t, h in enumerate(halves)
        ]

    @pl.when(j < count)
    def _():
        for c in copies(lax.rem(j, 2)):
            c.start()

    @pl.when(j > 0)
    def _():
        slot = lax.rem(j + 1, 2)
        rows = x_ref.shape[0]
        gate = up = jnp.zeros((rows, 256), f32)
        for i in range(0, depth, piece):
            sides = [
                split_rows(flat[slot, t, i : i + piece], flat[slot, t, depth + i : depth + i + piece])
                for t in range(2)
            ]
            x = x_ref[:, i : i + piece]
            gate += jnp.dot(
                x, jnp.concatenate([s[0] for s in sides], 1), preferred_element_type=f32
            )
            up += jnp.dot(x, jnp.concatenate([s[1] for s in sides], 1), preferred_element_type=f32)
        low = 0
        for ref, high in zip(outs, cuts):
            ref[0] = gate[low:high].astype(bf16)
            ref[1] = up[low:high].astype(bf16)
            low = high

    @pl.when(j < count)
    def _():
        for c in copies(lax.rem(j, 2)):
            c.wait()


def product(x, weights, first, last, cuts, *tokens):
    rows, depth = x.shape
    count = last - first
    sizes = [high - low for low, high in zip((0,) + cuts[:-1], cuts)]
    return pl.pallas_call(
        functools.partial(product_kernel, count=count, cuts=cuts),
        grid=(count + 1,),
        in_specs=[pl.BlockSpec(memory_space=pl.ANY)] * len(tokens)
        + [
            pl.BlockSpec((rows, depth), lambda j: (0, 0)),
            pl.BlockSpec(
                (depth, 1, 2, 128), lambda j: (0, 2 * (first + jnp.minimum(j, count - 1)), 0, 0)
            ),
            pl.BlockSpec(
                (depth, 1, 2, 128), lambda j: (0, 2 * (first + jnp.minimum(j, count - 1)) + 1, 0, 0)
            ),
        ],
        out_specs=[
            pl.BlockSpec((2, size, 256), lambda j: (0, 0, jnp.maximum(j - 1, 0))) for size in sizes
        ],
        out_shape=[jax.ShapeDtypeStruct((2, size, count * 256), bf16) for size in sizes],
        scratch_shapes=[
            pltpu.VMEM((2, 2, 2 * depth, 128), bf16),
            pltpu.SemaphoreType.DMA((2, 2)),
        ],
        compiler_params=pltpu.CompilerParams(vmem_limit_bytes=48 << 20),
        cost_estimate=SHORT,
    )(*tokens, x, weights, weights)


def gated_kernel(swap_ref, held_ref, kept_ref, near_ref, far_ref, out_ref):
    half = near_ref.shape[1]
    for i, theirs in enumerate((near_ref, far_ref)):
        rows = slice(i * half, (i + 1) * half)
        gate = kept_ref[0, rows].astype(f32) + theirs[0].astype(f32)
        up = kept_ref[1, rows].astype(f32) + theirs[1].astype(f32)
        start = jnp.bitwise_xor(swap_ref[0], i) * half
        out_ref[pl.ds(pl.multiple_of(start, half), half), :] = (jax.nn.silu(gate) * up).astype(bf16)


def gated(kept, near, far, swap, held, first, width):
    rows, half, columns = kept.shape[1], near.shape[1], kept.shape[2]
    wide = 512 if columns % 512 == 0 and first % 2 == 0 else 256
    return pl.pallas_call(
        gated_kernel,
        grid_spec=pltpu.PrefetchScalarGridSpec(
            num_scalar_prefetch=1,
            grid=(columns // wide,),
            in_specs=[
                pl.BlockSpec(memory_space=pl.ANY),
                pl.BlockSpec((2, rows, wide), lambda j, _: (0, 0, j)),
                pl.BlockSpec((2, half, wide), lambda j, _: (0, 0, j)),
                pl.BlockSpec((2, half, wide), lambda j, _: (0, 0, j)),
            ],
            out_specs=pl.BlockSpec((rows, wide), lambda j, _: (0, first * 256 // wide + j)),
        ),
        out_shape=jax.ShapeDtypeStruct((rows, width), bf16),
        input_output_aliases={} if held is None else {1: 0},
        cost_estimate=SHORT,
    )(swap, kept if held is None else held, kept, near, far)


def merge(terms):
    top = functools.reduce(jnp.maximum, [t[1] for t in terms])
    scales = [jnp.exp(t[1] - top) for t in terms]
    num = sum(t[0].astype(f32) * s[..., None] for t, s in zip(terms, scales))
    den = sum(t[2] * s for t, s in zip(terms, scales))
    return num, top, den


def new_token_terms(q, new_kv, kv_head, steps):
    sequences = q.shape[0]
    units = new_kv.reshape(steps, sequences, 2 * KVH, HD)
    keys = lax.dynamic_index_in_dim(units, kv_head, 2, False).astype(f32)
    values = lax.dynamic_index_in_dim(units, kv_head + KVH, 2, False).astype(f32)
    heads = q.shape[1] // steps
    step_of = jnp.arange(q.shape[1], dtype=jnp.int32) // heads
    qf = q.astype(f32)
    scores = [
        jnp.sum(qf * keys[t][:, None, :], axis=-1) * (1.0 / math.sqrt(HD)) for t in range(steps)
    ]
    scores = [jnp.where(t <= step_of[None, :], s, lowest) for t, s in enumerate(scores)]
    top = functools.reduce(jnp.maximum, scores)
    probs = [
        jnp.where(t <= step_of[None, :], jnp.exp(s - top), 0.0) for t, s in enumerate(scores)
    ]
    num = sum(
        p.astype(bf16).astype(f32)[..., None] * values[t][:, None, :] for t, p in enumerate(probs)
    )
    return num, top, sum(probs)


def on_device(prompt_rows, gate_up, queries, new_kv, kv_cache, lengths):
    gx, gy, gz = (lax.axis_index(a) for a in ("gx", "gy", "gz"))
    chips = lax.axis_size("gx")
    cores = lax.axis_size("gz")
    depth, _, width = gate_up.shape
    block = prompt_rows.shape[0]
    to_send = (gx // 2) != gy

    mine = interleave_lanes(prompt_rows)
    over_two = lax.ppermute(mine, "gx", xor_pairs("gx", 2))
    send_near = jnp.where(to_send, mine, over_two)
    own_near = jnp.where(to_send, over_two, mine)
    send_far = lax.ppermute(send_near, "gx", xor_pairs("gx", 1))
    own_far = lax.ppermute(own_near, "gx", xor_pairs("gx", 1))
    x1 = jnp.concatenate(both_cores(send_near), axis=0)
    x2 = jnp.concatenate(
        both_cores(send_far) + both_cores(own_near) + both_cores(own_far), axis=0
    )

    steps = queries.shape[0]
    sequences, slots = kv_cache.shape[:2]
    members = chips * cores
    me = gx * cores + gz
    heads = queries.shape[2] // HD
    my_q = queries.reshape(steps, sequences, heads, HD).transpose(1, 0, 2, 3)
    my_q = my_q.reshape(sequences, steps * heads, HD)
    late = over_two[0, 0]
    queued = my_q + jnp.where(late != late, late, jnp.zeros_like(late))
    all_q = lax.all_gather(queued, ("gx", "gz"), axis=0)

    weights = gate_up.reshape(depth, 2, width // 128, 128).transpose(0, 2, 1, 3)
    pairs = width // 256
    cuts = [0, pairs // 14 * 4, pairs // 14 * 10, pairs] if pairs % 14 == 0 else [0, pairs]
    spans = list(zip(cuts[:-1], cuts[1:]))
    over = [(0, 1), (1, 0)]
    half = cores * block
    near, tokens = [], ()
    for first, last in spans:
        (out,) = product(x1, weights, first, last, (half,), *tokens)
        near.append(lax.ppermute(out, "gy", over))
        tokens = (out,)
    limits = jnp.clip(lengths - me * slots, 0, slots)
    kept, far = [], []
    for i, (first, last) in enumerate(spans):
        arrived = far[i - 2] if i >= 2 else near[i]
        if i == len(spans) - 1:
            num, stat = cached_attention(all_q, kv_cache, limits, *tokens, near[-1])
            tokens = (num,)
        sent, keep = product(x2, weights, first, last, (half, 3 * half), *tokens, arrived)
        far.append(lax.ppermute(sent, "gy", over))
        kept.append(keep)
        tokens = (keep,)
    swap = (gx % 2).reshape(1)
    hidden_units = None
    for i, (first, last) in enumerate(spans):
        hidden_units = gated(kept[i], near[i], far[i], swap, hidden_units, first, width)

    rows = steps * heads
    num = num.reshape(chips, cores, sequences, rows, HD)
    stat = stat.reshape(2, sequences, chips, cores, rows).transpose(2, 3, 0, 1, 4)
    keep_num = lax.dynamic_index_in_dim(num, gz, 1, False)
    give_num = lax.dynamic_index_in_dim(num, 1 - gz, 1, False)
    keep_stat = lax.dynamic_index_in_dim(stat, gz, 1, False)
    give_stat = lax.dynamic_index_in_dim(stat, 1 - gz, 1, False)
    got_num = lax.ppermute(give_num, "gz", over)
    got_stat = lax.ppermute(give_stat, "gz", over)
    pair_num, pair_top, pair_den = merge(
        [(keep_num, keep_stat[:, 0], keep_stat[:, 1]), (got_num, got_stat[:, 0], got_stat[:, 1])]
    )
    pair_num = pair_num.astype(bf16)
    pair_stat = jnp.stack([pair_top, pair_den], axis=1)
    terms = []
    for bit in range(chips):
        n = lax.dynamic_index_in_dim(pair_num, gx ^ bit, 0, False)
        s = lax.dynamic_index_in_dim(pair_stat, gx ^ bit, 0, False)
        if bit:
            n = lax.ppermute(n, "gx", xor_pairs("gx", bit))
            s = lax.ppermute(s, "gx", xor_pairs("gx", bit))
        terms.append((n, s[0], s[1]))
    terms.append(new_token_terms(my_q, new_kv, me * KVH // members, steps))
    num, _, den = merge(terms)
    attended = (num / den[..., None]).astype(bf16)
    attended = attended.reshape(sequences, steps, heads, HD).transpose(1, 0, 2, 3)
    return hidden_units, attended.reshape(steps, sequences, heads * HD)


def plain_on_device(prompt_rows, gate_up, queries, new_kv, kv_cache, lengths):
    partial_terms = jnp.dot(
        lax.all_gather(prompt_rows, ("gx", "gz"), axis=0, tiled=True),
        gate_up.reshape(gate_up.shape[0], -1),
        preferred_element_type=f32,
    )
    summed = lax.psum_scatter(
        partial_terms.astype(bf16), "gy", scatter_dimension=0, tiled=True
    ).astype(f32)
    summed = summed.reshape(summed.shape[0], 2, -1)
    hidden_units = (jax.nn.silu(summed[:, 0]) * summed[:, 1]).astype(bf16)
    members = lax.axis_size(("gx", "gz"))
    me = lax.axis_index(("gx", "gz"))
    steps = queries.shape[0]
    sequences, slots = kv_cache.shape[:2]
    all_q = lax.all_gather(queries, ("gx", "gz"), axis=2, tiled=True)
    grouped = all_q.reshape(steps, sequences, KVH, -1, HD)
    cache = kv_cache.reshape(sequences, slots, 2, KVH, HD)
    fresh = new_kv.reshape(steps, sequences, 2, KVH, HD).transpose(1, 0, 2, 3, 4)
    units = jnp.concatenate([cache, fresh], axis=1)
    scores = jnp.einsum(
        "sukgd,ujkd->sukgj", grouped, units[:, :, 0], preferred_element_type=f32
    ) * (1.0 / math.sqrt(HD))
    cached = me * slots + jnp.arange(slots, dtype=jnp.int32)[None, :] < lengths[:, None]
    ids = jnp.arange(steps, dtype=jnp.int32)
    fresh_seen = (ids[None, :] <= ids[:, None]) & (me == 0)
    seen = jnp.concatenate(
        [
            jnp.broadcast_to(cached[None], (steps, sequences, slots)),
            jnp.broadcast_to(fresh_seen[:, None, :], (steps, sequences, steps)),
        ],
        axis=2,
    )[:, :, None, None, :]
    masked = jnp.where(seen, scores, lowest)
    top = jnp.max(masked, axis=-1)
    probs = jnp.where(seen, jnp.exp(masked - top[..., None]), 0.0)
    den = jnp.sum(probs, axis=-1)
    num = jnp.einsum(
        "sukgj,ujkd->sukgd", probs.astype(bf16), units[:, :, 1], preferred_element_type=f32
    )
    overall = lax.pmax(top, ("gx", "gz"))
    scale = jnp.exp(top - overall)
    num = (num * scale[..., None]).reshape(steps, sequences, -1, HD)
    den = (den * scale).reshape(steps, sequences, -1)
    num = lax.psum_scatter(
        num.astype(bf16), ("gx", "gz"), scatter_dimension=2, tiled=True
    ).astype(f32)
    den = lax.psum_scatter(den, ("gx", "gz"), scatter_dimension=2, tiled=True)
    attended = (num / den[..., None]).astype(bf16)
    return hidden_units, attended.reshape(steps, sequences, -1)


def solution(mesh):
    sizes = mesh.shape
    paired = sizes["gy"] == 2 and sizes["gx"] == KVH and sizes["gz"] == 2
    return jax.shard_map(
        on_device if paired else plain_on_device,
        mesh=mesh,
        in_specs=(
            P(("groups", "gx", "gz"), "gy"),
            P("gy", None, ("gx", "gz")),
            P(None, ("groups", "gy"), ("gx", "gz")),
            P(None, ("groups", "gy"), None),
            P(("groups", "gy"), ("gx", "gz"), None),
            P(("groups", "gy")),
        ),
        out_specs=(P(("groups", "gy"), ("gx", "gz")), P(None, ("groups", "gy"), ("gx", "gz"))),
        check_vma=False,
    )
```

time: 283 us -> 203 us (0.72)
  Pallas kernels: 0 us -> 108 us
  local copies, waits for them, and re-layouts: 107 us -> 12.1 us
  matrix products: 52.1 us -> 0 us
  blocking collectives: 30.4 us -> 0 us
  starting transfers between devices: 0.34 us -> 22.1 us
  waiting for transfers between devices: 51.3 us -> 33.3 us
  other arithmetic: 26.6 us -> 9.82 us
    pallas_call x0 -> x11, Pallas kernels: none -> 108 us  [the longest x6 80.7 us: product(): pl.pallas_call(functools.partial(product_kernel, count=count, cuts=cuts),...]
    unnamed x7 -> x37, local copies, waits for them, and re-layouts: 64.3 us -> 7.92 us
    dot_general x3 -> x0, matrix products: 52.1 us -> none  [the longest x1 38.9 us: on_device(): jnp.dot(lax.all_gather(prompt_rows, ('gx', 'gz'), axis=0, tiled=True), fl...]
    reduce_scatter x1 -> x0, waiting for transfers between devices: 49.8 us -> none  [on_device(): lax.psum_scatter(partial_terms.astype(jnp.bfloat16), 'gy', scatter_dimens...]
    ppermute x0 -> x21, waiting for transfers between devices: none -> 33.3 us  [the longest x1 20.6 us: on_device(): over_two = lax.ppermute(mine, 'gx', xor_pairs('gx', 2))]
    reshape x4 -> x1, local copies, waits for them, and re-layouts: 32.2 us -> 0.71 us  [on_device(): return (hidden_units, attended.reshape(steps, sequences, heads * HD))]
    all_gather x2 -> x0, blocking collectives: 30.4 us -> none  [joined(): lax.all_gather(a.astype(kind), axis)]
    ppermute x0 -> x21, starting transfers between devices: none -> 22.1 us  [the longest x3 4.45 us: on_device(): s = lax.ppermute(s, 'gx', xor_pairs('gx', bit))]
  transfers between devices with their start and end apart: 4 -> 22, of which waited for: 1 -> 5; matrix products, arithmetic and copies ran while one was open for 59% -> 6% of each run, Pallas kernels for 0% -> 52%
where the time goes in v1:
time: 203 us; the launch traced here: 202 us
  Pallas kernels  108 us (53%)
  waiting for transfers between devices  33.3 us (16%)
  starting transfers between devices  22.1 us (11%)
  between operations  16.5 us (8%)
  local copies, waits for them, and re-layouts  12.1 us (6%)
  other arithmetic  9.82 us (5%)
    pallas_call x6, Pallas kernels, product(): pl.pallas_call(functools.partial(product_kernel, count=count, cuts=cuts),...  80.7 us
    ppermute x1, waiting for transfers between devices, on_device(): over_two = lax.ppermute(mine, 'gx', xor_pairs('gx', 2))  20.6 us
    pallas_call x1, Pallas kernels, cached_attention(): pl.pallas_call(functools.partial(attention_kernel, per_step=per_step, mem...  16.9 us
    ppermute x1, waiting for transfers between devices, on_device(): send_far = lax.ppermute(send_near, 'gx', xor_pairs('gx', 1))  8.59 us
    pallas_call x3, Pallas kernels, gated(): pl.pallas_call(gated_kernel, grid_spec=pltpu.PrefetchScalarGridSpec(num_s...  8.5 us
    unnamed x37, local copies, waits for them, and re-layouts  7.92 us
    unnamed x5, other arithmetic  4.83 us
    ppermute x3, starting transfers between devices, on_device(): s = lax.ppermute(s, 'gx', xor_pairs('gx', bit))  4.45 us
  transfers between devices with their start and end apart: 22, of which 5 were waited for; matrix products, arithmetic and copies ran while one was open for 6% of the time, Pallas kernels for 52%

profile of v1, /device:TPU:0, one launch (start us, length us, event | category | flops | bytes accessed | tf_op | source)
XLA Modules:
  0.0 202.3 jit_solution(1976394937208479320)
XLA Ops:
  7.2 2.4 %shard_map.77 = bf16[64,4096]{1,0:T(8,128)(2,1)} custom-call(bf16[64,4096]{1,0:T(8,128)(2,1)} %x_ref.1), custom_call_target="tpu_custom_call" | custom-call | flops 1 | bytes 1 | tf_op jit(solution)/shard_map/pallas_call | solution.py:106
  9.6 4.0 %collective-permute-start = (bf16[64,4096]{1,0:T(8,128)(2,1)}, bf16[64,4096]{1,0:T(8,128)(2,1)S(1)}, u32[]{:S(2)}, u32[]{:S(2)}) collective-permute-start(bf16[64,4096]{1,0:T(8,128)(2,1)} %shard_map.77), channel_id=1, source_target_pairs={{0,8},{4,12},{8,0},{12,4},{1,9},{5,13},{9,1},{13,5},{2,10},{6,14},... | collective-permute-start | bytes 1572872 | tf_op jit(solution)/shard_map/ppermute | solution.py:270
  13.6 0.9 copy.51
  14.5 0.9 copy.50
  15.6 0.6 fusion.30
  16.4 20.6 %collective-permute-done = bf16[64,4096]{1,0:T(8,128)(2,1)S(1)} collective-permute-done((bf16[64,4096]{1,0:T(8,128)(2,1)}, bf16[64,4096]{1,0:T(8,128)(2,1)S(1)}, u32[]{:S(2)}, u32[]{:S(2)}) %collective-permute-start) | collective-permute-done | bytes 524320 | tf_op jit(solution)/shard_map/ppermute | solution.py:270
  37.0 1.9 broadcast_select_fusion
  38.9 0.8 collective-permute-start.3
  39.7 0.7 copy.37
  40.6 1.2 collective-permute-start.6
  44.3 0.7 copy_bitcast_fusion.1
  45.0 8.6 %collective-permute-done.3 = bf16[64,4096]{1,0:T(8,128)(2,1)S(1)} collective-permute-done((bf16[64,4096]{1,0:T(8,128)(2,1)S(1)}, bf16[64,4096]{1,0:T(8,128)(2,1)S(1)}, u32[]{:S(2)}, u32[]{:S(2)}) %collective-permute-start.3) | collective-permute-done | bytes 524320 | tf_op jit(solution)/shard_map/ppermute | solution.py:273
  53.8 10.6 %shard_map.78.refs_0_ = bf16[2,128,1024]{2,1,0:T(8,128)(2,1)} custom-call(bf16[128,4096]{1,0:T(8,128)(2,1)S(1)} %pad_maximum_fusion.refs_0_.refs_1_, bf16[4096,28,2,128]{3,2,1,0:T(2,128)(2,1)} %bitcast.200, bf16[4096,28,2,128]{3,2,1,0:T(2,128)(2,1)} %bitcast.201), custom_call_target="tpu_custom_call" | custom-call | flops 1 | bytes 1 | tf_op jit(solution)/shard_map/pallas_call | solution.py:173
  64.4 14.5 %shard_map.79.refs_0_ = bf16[2,128,1536]{2,1,0:T(8,128)(2,1)} custom-call(bf16[2,128,1024]{2,1,0:T(8,128)(2,1)} %shard_map.78.refs_0_, bf16[128,4096]{1,0:T(8,128)(2,1)S(1)} %pad_maximum_fusion.refs_0_.refs_1_, bf16[4096,28,2,128]{3,2,1,0:T(2,128)(2,1)} %bitcast.202, bf16[4096,28,2,128]{3,2,1,0:T(2,128)(2,1)} %bitcast.203), custom_call_target="tpu_custom_call" | custom-call | flops 1 | bytes 1 | tf_op jit(solution)/shard_map/pallas_call | solution.py:173
  78.9 1.6 collective-permute-start.2
  80.5 10.6 %shard_map.80.refs_0_ = bf16[2,128,1024]{2,1,0:T(8,128)(2,1)} custom-call(bf16[2,128,1536]{2,1,0:T(8,128)(2,1)} %shard_map.79.refs_0_, bf16[128,4096]{1,0:T(8,128)(2,1)S(1)} %pad_maximum_fusion.refs_0_.refs_1_, bf16[4096,28,2,128]{3,2,1,0:T(2,128)(2,1)} %bitcast.204, bf16[4096,28,2,128]{3,2,1,0:T(2,128)(2,1)} %bitcast.205), custom_call_target="tpu_custom_call" | custom-call | flops 1 | bytes 1 | tf_op jit(solution)/shard_map/pallas_call | solution.py:173
  91.2 0.5 collective-permute-start.9
  91.7 1.6 collective-permute-start.11
  93.4 1.2 select_dynamic-update-slice_fusion.4
  94.6 1.2 select_dynamic-update-slice_fusion.3
  95.8 1.2 select_dynamic-update-slice_fusion.2
  97.0 1.2 select_dynamic-update-slice_fusion.1
  98.3 14.0 %shard_map.81 = (bf16[2,128,1024]{2,1,0:T(8,128)(2,1)}, bf16[2,256,1024]{2,1,0:T(8,128)(2,1)S(1)}) custom-call(bf16[2,128,1024]{2,1,0:T(8,128)(2,1)} %shard_map.80.refs_0_, bf16[2,128,1024]{2,1,0:T(8,128)(2,1)S(1)} %collective-permute-done.2.refs_1_.near_ref, bf16[384,4096]{1,0:T(8,128)(2,1)S(1)} %select_dynamic-update-slice_fusion.refs_2_, ...), custom_call_target="tpu_custom_call" | custom-call | flops 1 | bytes 1 | tf_op jit(solution)/shard_map/pallas_call | solution.py:173
  112.3 1.0 copy-done.1
  113.9 1.2 copy-done.2
  115.1 18.0 %shard_map.83 = (bf16[2,128,1536]{2,1,0:T(8,128)(2,1)}, bf16[2,256,1536]{2,1,0:T(8,128)(2,1)S(1)}) custom-call(bf16[2,256,1024]{2,1,0:T(8,128)(2,1)S(1)} %copy-done.2, bf16[2,128,1536]{2,1,0:T(8,128)(2,1)} %collective-permute-done.9.refs_1_.near_ref, bf16[384,4096]{1,0:T(8,128)(2,1)} %copy-done, bf16[4096,28,2,128]{3,2,1,0:T(2,128)(2,1)} %bitcast.208, ...), custom_call_target="tpu_custom_call" | custom-call | flops 1 | bytes 1 | tf_op jit(solution)/shard_map/pallas_call | solution.py:173
  133.1 1.6 collective-permute-start.10
  134.8 0.8 copy-done.5
  135.6 2.4 %shard_map.82.held_ref = bf16[256,3584]{1,0:T(8,128)(2,1)} custom-call(s32[1]{0:T(128)} %bitcast.swap_ref, bf16[2,256,1024]{2,1,0:T(8,128)(2,1)} %copy-done.1, bf16[2,256,1024]{2,1,0:T(8,128)(2,1)} %copy-done.1, bf16[2,128,1024]{2,1,0:T(8,128)(2,1)} %copy-done.4, bf16[2,128,1024]{2,1,0:T(8,128)(2,1)} %copy-done.5), custom_call_target="tpu_custom_call" | custom-call | flops 1 | bytes 1 | tf_op jit(solution)/shard_map/pallas_call | solution.py:212
  138.0 1.2 copy-done.7
  139.2 16.9 %shard_map.85 = (bf16[8,32,16,128]{3,2,1,0:T(8,128)(2,1)S(1)}, f32[2,32,128]{2,1,0:T(8,128)S(1)}) custom-call(s32[32]{0:T(128)S(1)} %subtract_clamp_fusion.limits_ref, bf16[2,256,1536]{2,1,0:T(8,128)(2,1)S(1)} %get-tuple-element.12.kept_ref.refs_0_, bf16[2,128,1024]{2,1,0:T(8,128)(2,1)} %collective-permute-done.11.refs_1_.near_ref, ...), custom_call_target="tpu_custom_call" | custom-call | flops 1 | bytes 1 | tf_op jit(solution)/shard_map/pallas_call | solution.py:67
  156.4 0.5 collective-permute-start.14
  156.9 13.0 %shard_map.86 = (bf16[2,128,1024]{2,1,0:T(8,128)(2,1)S(1)}, bf16[2,256,1024]{2,1,0:T(8,128)(2,1)S(1)}) custom-call(bf16[8,32,16,128]{3,2,1,0:T(8,128)(2,1)S(1)} %get-tuple-element.14.refs_0_, bf16[2,128,1024]{2,1,0:T(8,128)(2,1)S(1)} %copy-done.6, bf16[384,4096]{1,0:T(8,128)(2,1)} %copy-done, bf16[4096,28,2,128]{3,2,1,0:T(2,128)(2,1)} %bitcast.210, ...), custom_call_target="tpu_custom_call" | custom-call | flops 1 | bytes 1 | tf_op jit(solution)/shard_map/pallas_call | solution.py:173
  170.0 1.0 copy-done.8
  171.0 3.6 %collective-permute-start.17 = (f32[2,32,16]{1,2,0:T(8,128)S(1)}, f32[2,32,16]{1,2,0:T(8,128)S(1)}, u32[]{:S(2)}, u32[]{:S(2)}) collective-permute-start(f32[2,32,16]{1,2,0:T(8,128)S(1)} %get-tuple-element.44), channel_id=1, source_target_pairs={{0,12},{4,8},{8,4},{12,0},{1,13},{5,9},{9,5},{13,1},{2,14},{6,10},... | collective-permute-start | bytes 12296 | tf_op jit(solution)/shard_map/ppermute | solution.py:338
  174.6 0.9 collective-permute-start.15
  175.7 1.0 collective-permute-done.17
  177.1 2.1 %collective-permute-done.16 = f32[2,32,16]{1,2,0:T(8,128)S(1)} collective-permute-done((f32[2,32,16]{1,2,0:T(8,128)S(1)}, f32[2,32,16]{1,2,0:T(8,128)S(1)}, u32[]{:S(2)}, u32[]{:S(2)}) %collective-permute-start.16) | collective-permute-done | bytes 4128 | tf_op jit(solution)/shard_map/ppermute | solution.py:338
  179.3 1.7 fusion.1
  181.0 1.5 collective-permute-start.20
  182.6 0.6 collective-permute-start.19
  183.2 2.3 %collective-permute-start.18 = (bf16[32,16,128]{2,1,0:T(8,128)(2,1)S(1)}, bf16[32,16,128]{2,1,0:T(8,128)(2,1)S(1)}, u32[]{:S(2)}, u32[]{:S(2)}) collective-permute-start(bf16[32,16,128]{2,1,0:T(8,128)(2,1)S(1)} %get-tuple-element.33), channel_id=1, source_target_pairs={{0,4},{4,0},{8,12},{12,8},{1,5},{5,1},{9,13},{13,9},{2,6},{6,2},{1... | collective-permute-start | bytes 393224 | tf_op jit(solution)/shard_map/ppermute | solution.py:337
  186.2 3.7 %shard_map.84.held_ref = bf16[256,3584]{1,0:T(8,128)(2,1)} custom-call(s32[1]{0:T(128)} %bitcast.swap_ref, bf16[256,3584]{1,0:T(8,128)(2,1)} %shard_map.82.held_ref, bf16[2,256,1536]{2,1,0:T(8,128)(2,1)} %copy-done.3, bf16[2,128,1536]{2,1,0:T(8,128)(2,1)} %collective-permute-done.9.refs_1_.near_ref, ...), custom_call_target="tpu_custom_call", output_to_operand_aliasing={{}: (1, {})} | custom-call | flops 1 | bytes 1 | tf_op jit(solution)/shard_map/pallas_call | solution.py:212
  189.9 0.8 copy-done.11
  190.7 2.4 %shard_map.87 = bf16[256,3584]{1,0:T(8,128)(2,1)} custom-call(s32[1]{0:T(128)} %bitcast.swap_ref, bf16[256,3584]{1,0:T(8,128)(2,1)} %shard_map.84.held_ref, bf16[2,256,1024]{2,1,0:T(8,128)(2,1)} %copy-done.8, bf16[2,128,1024]{2,1,0:T(8,128)(2,1)} %collective-permute-done.11.refs_1_.near_ref, ...), custom_call_target="tpu_custom_call", output_to_operand_aliasing={{}: (1, {})} | custom-call | flops 1 | bytes 1 | tf_op jit(solution)/shard_map/pallas_call | solution.py:212
  193.1 1.0 collective-permute-done.19
  194.1 0.6 copy_bitcast_fusion
  194.8 0.7 reshape.578
  (88 shorter events, 3.8 us)
Async XLA Ops:
  7.2 37.1 %copy-start.12 = (bf16[2,32,1024]{2,1,0:T(8,128)(2,1)S(1)}, bf16[2,32,1024]{2,1,0:T(8,128)(2,1)}, u32[]{:S(2)}) copy-start(bf16[2,32,1024]{2,1,0:T(8,128)(2,1)} %param.8) | copy-start | bytes 393220
  7.2 130.8 %all-gather.2.cloned.1.call-start = ((), (), s32[]{:S(2)}) async-start(), calls=%async_computation | async-start | bytes 1179648 | tf_op jit(solution)/shard_map/all_gather | solution.py:289
  9.6 27.4 %collective-permute-start = (bf16[64,4096]{1,0:T(8,128)(2,1)}, bf16[64,4096]{1,0:T(8,128)(2,1)S(1)}, u32[]{:S(2)}, u32[]{:S(2)}) collective-permute-start(bf16[64,4096]{1,0:T(8,128)(2,1)} %shard_map.77), channel_id=1, source_target_pairs={{0,8},{4,12},{8,0},{12,4},{1,9},{5,13},{9,1},{13,5},{2,10},{6,14},... | collective-permute-start | bytes 1572872 | tf_op jit(solution)/shard_map/ppermute | solution.py:270
  38.9 14.7 %collective-permute-start.1 = (bf16[64,4096]{1,0:T(8,128)(2,1)S(1)}, bf16[64,4096]{1,0:T(8,128)(2,1)S(1)}, u32[]{:S(2)}, u32[]{:S(2)}) collective-permute-start(bf16[64,4096]{1,0:T(8,128)(2,1)S(1)} %get-tuple-element.30), channel_id=1, source_target_pairs={{0,1},{1,0},{2,3},{3,2},{4,5},{5,4},{6,7},{7,6},{8,9},{9,8},{10,11... | collective-permute-start | bytes 1572872 | tf_op jit(solution)/shard_map/ppermute | solution.py:24
  38.9 14.7 %collective-permute-start.3 = (bf16[64,4096]{1,0:T(8,128)(2,1)S(1)}, bf16[64,4096]{1,0:T(8,128)(2,1)S(1)}, u32[]{:S(2)}, u32[]{:S(2)}) collective-permute-start(bf16[64,4096]{1,0:T(8,128)(2,1)S(1)} %get-tuple-element.30), channel_id=1, source_target_pairs={{0,4},{4,0},{8,12},{12,8},{1,5},{5,1},{9,13},{13,9},{2,6},{6,2},{1... | collective-permute-start | bytes 1572872 | tf_op jit(solution)/shard_map/ppermute | solution.py:273
  40.4 54.2 %collective-permute-start.5 = (bf16[64,4096]{1,0:T(8,128)(2,1)}, bf16[64,4096]{1,0:T(8,128)(2,1)}, u32[]{:S(2)}, u32[]{:S(2)}) collective-permute-start(bf16[64,4096]{1,0:T(8,128)(2,1)} %get-tuple-element.29), channel_id=1, source_target_pairs={{0,1},{1,0},{2,3},{3,2},{4,5},{5,4},{6,7},{7,6},{8,9},{9,8},{10,11... | collective-permute-start | bytes 1572872 | tf_op jit(solution)/shard_map/ppermute | solution.py:24
  40.6 51.1 %collective-permute-start.6 = (bf16[64,4096]{1,0:T(8,128)(2,1)}, bf16[64,4096]{1,0:T(8,128)(2,1)}, u32[]{:S(2)}, u32[]{:S(2)}) collective-permute-start(bf16[64,4096]{1,0:T(8,128)(2,1)} %get-tuple-element.29), channel_id=1, source_target_pairs={{0,4},{4,0},{8,12},{12,8},{1,5},{5,1},{9,13},{13,9},{2,6},{6,2},{1... | collective-permute-start | bytes 1572872 | tf_op jit(solution)/shard_map/ppermute | solution.py:274
  53.6 10.8 %copy-start.9 = (bf16[64,4096]{1,0:T(8,128)(2,1)}, bf16[64,4096]{1,0:T(8,128)(2,1)S(1)}, u32[]{:S(2)}) copy-start(bf16[64,4096]{1,0:T(8,128)(2,1)S(1)} %collective-permute-done.3) | copy-start | bytes 1572868
  53.6 39.7 %collective-permute-start.4 = (bf16[64,4096]{1,0:T(8,128)(2,1)S(1)}, bf16[64,4096]{1,0:T(8,128)(2,1)}, u32[]{:S(2)}, u32[]{:S(2)}) collective-permute-start(bf16[64,4096]{1,0:T(8,128)(2,1)S(1)} %collective-permute-done.3), channel_id=1, source_target_pairs={{0,1},{1,0},{2,3},{3,2},{4,5},{5,4},{6,7},{7,6},{8,9},{9,8},{10,11... | collective-permute-start | bytes 1572872 | tf_op jit(solution)/shard_map/ppermute | solution.py:24
  78.9 14.4 %copy-start.10 = (bf16[64,4096]{1,0:T(8,128)(2,1)S(1)}, bf16[64,4096]{1,0:T(8,128)(2,1)}, u32[]{:S(2)}) copy-start(bf16[64,4096]{1,0:T(8,128)(2,1)} %copy-done.9) | copy-start | bytes 1572868
  78.9 19.4 %collective-permute-start.2 = (bf16[2,128,1024]{2,1,0:T(8,128)(2,1)}, bf16[2,128,1024]{2,1,0:T(8,128)(2,1)S(1)}, u32[]{:S(2)}, u32[]{:S(2)}) collective-permute-start(bf16[2,128,1024]{2,1,0:T(8,128)(2,1)} %shard_map.78.refs_0_), channel_id=1, source_target_pairs={{0,2},{2,0},{1,3},{3,1},{4,6},{6,4},{5,7},{7,5},{8,10},{10,8},{9,1... | collective-permute-start | bytes 1572872 | tf_op jit(solution)/shard_map/ppermute | solution.py:300
  91.2 22.7 %collective-permute-start.9 = (bf16[2,128,1536]{2,1,0:T(8,128)(2,1)}, bf16[2,128,1536]{2,1,0:T(8,128)(2,1)}, u32[]{:S(2)}, u32[]{:S(2)}) collective-permute-start(bf16[2,128,1536]{2,1,0:T(8,128)(2,1)} %shard_map.79.refs_0_), channel_id=1, source_target_pairs={{0,2},{2,0},{1,3},{3,1},{4,6},{6,4},{5,7},{7,5},{8,10},{10,8},{9,1... | collective-permute-start | bytes 2359304 | tf_op jit(solution)/shard_map/ppermute | solution.py:300
  91.7 46.3 %collective-permute-start.11 = (bf16[2,128,1024]{2,1,0:T(8,128)(2,1)}, bf16[2,128,1024]{2,1,0:T(8,128)(2,1)}, u32[]{:S(2)}, u32[]{:S(2)}) collective-permute-start(bf16[2,128,1024]{2,1,0:T(8,128)(2,1)} %shard_map.80.refs_0_), channel_id=1, source_target_pairs={{0,2},{2,0},{1,3},{3,1},{4,6},{6,4},{5,7},{7,5},{8,10},{10,8},{9,1... | collective-permute-start | bytes 1572872 | tf_op jit(solution)/shard_map/ppermute | solution.py:300
  93.3 3.7 %collective-permute-start.7 = (bf16[64,4096]{1,0:T(8,128)(2,1)}, bf16[64,4096]{1,0:T(8,128)(2,1)S(1)}, u32[]{:S(2)}, u32[]{:S(2)}) collective-permute-start(bf16[64,4096]{1,0:T(8,128)(2,1)} %collective-permute-done.6), channel_id=1, source_target_pairs={{0,1},{1,0},{2,3},{3,2},{4,5},{5,4},{6,7},{7,6},{8,9},{9,8},{10,11... | collective-permute-start | bytes 1572872 | tf_op jit(solution)/shard_map/ppermute | solution.py:24
  98.3 14.0 %copy-start = (bf16[384,4096]{1,0:T(8,128)(2,1)}, bf16[384,4096]{1,0:T(8,128)(2,1)S(1)}, u32[]{:S(2)}) copy-start(bf16[384,4096]{1,0:T(8,128)(2,1)S(1)} %select_dynamic-update-slice_fusion.refs_2_) | copy-start | bytes 9437188
  98.3 15.5 %copy-start.16 = (s32[32]{0:T(128)S(1)}, s32[32]{0:T(128)}, u32[]{:S(2)}) copy-start(s32[32]{0:T(128)} %param.11) | copy-start | bytes 388
  98.3 14.0 %copy-start.4 = (bf16[2,128,1024]{2,1,0:T(8,128)(2,1)}, bf16[2,128,1024]{2,1,0:T(8,128)(2,1)S(1)}, u32[]{:S(2)}) copy-start(bf16[2,128,1024]{2,1,0:T(8,128)(2,1)S(1)} %collective-permute-done.2.refs_1_.near_ref) | copy-start | bytes 1572868
  112.3 1.0 copy-start.1
  113.3 21.5 %collective-permute-start.8 = (bf16[2,128,1024]{2,1,0:T(8,128)(2,1)}, bf16[2,128,1024]{2,1,0:T(8,128)(2,1)S(1)}, u32[]{:S(2)}, u32[]{:S(2)}) collective-permute-start(bf16[2,128,1024]{2,1,0:T(8,128)(2,1)} %get-tuple-element.11), channel_id=1, source_target_pairs={{0,2},{2,0},{1,3},{3,1},{4,6},{6,4},{5,7},{7,5},{8,10},{10,8},{9,1... | collective-permute-start | bytes 1572872 | tf_op jit(solution)/shard_map/ppermute | solution.py:310
  113.9 1.2 copy-start.2
  133.1 23.0 %copy-start.3 = (bf16[2,256,1536]{2,1,0:T(8,128)(2,1)}, bf16[2,256,1536]{2,1,0:T(8,128)(2,1)S(1)}, u32[]{:S(2)}) copy-start(bf16[2,256,1536]{2,1,0:T(8,128)(2,1)S(1)} %get-tuple-element.12.kept_ref.refs_0_) | copy-start | bytes 4718596
  133.1 53.0 %collective-permute-start.10 = (bf16[2,128,1536]{2,1,0:T(8,128)(2,1)}, bf16[2,128,1536]{2,1,0:T(8,128)(2,1)}, u32[]{:S(2)}, u32[]{:S(2)}) collective-permute-start(bf16[2,128,1536]{2,1,0:T(8,128)(2,1)} %get-tuple-element.13), channel_id=1, source_target_pairs={{0,2},{2,0},{1,3},{3,1},{4,6},{6,4},{5,7},{7,5},{8,10},{10,8},{9,1... | collective-permute-start | bytes 2359304 | tf_op jit(solution)/shard_map/ppermute | solution.py:310
  134.8 0.8 copy-start.5
  138.0 1.2 copy-start.7
  139.2 17.7 %copy-start.6 = (bf16[2,128,1024]{2,1,0:T(8,128)(2,1)S(1)}, bf16[2,128,1024]{2,1,0:T(8,128)(2,1)}, u32[]{:S(2)}) copy-start(bf16[2,128,1024]{2,1,0:T(8,128)(2,1)} %copy-done.5) | copy-start | bytes 1572868
  156.2 14.7 %collective-permute-start.13 = (f32[4,2,32,16]{2,3,0,1:T(8,128)S(1)}, f32[4,2,32,16]{2,3,0,1:T(8,128)S(1)}, u32[]{:S(2)}, u32[]{:S(2)}) collective-permute-start(f32[4,2,32,16]{2,3,0,1:T(8,128)S(1)} %get-tuple-element.41), channel_id=1, source_target_pairs={{0,1},{1,0},{2,3},{3,2},{4,5},{5,4},{6,7},{7,6},{8,9},{9,8},{10,11... | collective-permute-start | bytes 49160 | tf_op jit(solution)/shard_map/ppermute | solution.py:326
  156.4 22.9 %copy-start.13 = (f32[32,2,8]{0,2,1:T(8,128)S(1)}, f32[32,2,8]{0,2,1:T(8,128)}, u32[]{:S(2)}) copy-start(f32[32,2,8]{0,2,1:T(8,128)} %copy.37) | copy-start | bytes 6148
  156.4 22.9 %collective-permute-start.14 = (bf16[4,32,16,128]{3,2,1,0:T(8,128)(2,1)S(1)}, bf16[4,32,16,128]{3,2,1,0:T(8,128)(2,1)}, u32[]{:S(2)}, u32[]{:S(2)}) collective-permute-start(bf16[4,32,16,128]{3,2,1,0:T(8,128)(2,1)S(1)} %dynamic-slice_bitcast_fusion), channel_id=1, source_target_pairs={{0,1},{1,0},{2,3},{3,2},{4,5},{5,4},{6,7},{7,6},{8,9},{9,8},{10,11... | collective-permute-start | bytes 1572872 | tf_op jit(solution)/shard_map/ppermute | solution.py:325
  170.0 1.0 copy-start.8
  171.0 5.6 %collective-permute-start.17 = (f32[2,32,16]{1,2,0:T(8,128)S(1)}, f32[2,32,16]{1,2,0:T(8,128)S(1)}, u32[]{:S(2)}, u32[]{:S(2)}) collective-permute-start(f32[2,32,16]{1,2,0:T(8,128)S(1)} %get-tuple-element.44), channel_id=1, source_target_pairs={{0,12},{4,8},{8,4},{12,0},{1,13},{5,9},{9,5},{13,1},{2,14},{6,10},... | collective-permute-start | bytes 12296 | tf_op jit(solution)/shard_map/ppermute | solution.py:338
  174.6 4.6 %collective-permute-start.16 = (f32[2,32,16]{1,2,0:T(8,128)S(1)}, f32[2,32,16]{1,2,0:T(8,128)S(1)}, u32[]{:S(2)}, u32[]{:S(2)}) collective-permute-start(f32[2,32,16]{1,2,0:T(8,128)S(1)} %get-tuple-element.43), channel_id=1, source_target_pairs={{0,8},{4,12},{8,0},{12,4},{1,9},{5,13},{9,1},{13,5},{2,10},{6,14},... | collective-permute-start | bytes 12296 | tf_op jit(solution)/shard_map/ppermute | solution.py:338
  174.6 4.6 %collective-permute-start.15 = (f32[2,32,16]{1,2,0:T(8,128)S(1)}, f32[2,32,16]{1,2,0:T(8,128)S(1)}, u32[]{:S(2)}, u32[]{:S(2)}) collective-permute-start(f32[2,32,16]{1,2,0:T(8,128)S(1)} %get-tuple-element.45), channel_id=1, source_target_pairs={{0,4},{4,0},{8,12},{12,8},{1,5},{5,1},{9,13},{13,9},{2,6},{6,2},{1... | collective-permute-start | bytes 12296 | tf_op jit(solution)/shard_map/ppermute | solution.py:338
  176.6 13.3 %collective-permute-start.12 = (bf16[2,128,1024]{2,1,0:T(8,128)(2,1)S(1)}, bf16[2,128,1024]{2,1,0:T(8,128)(2,1)S(1)}, u32[]{:S(2)}, u32[]{:S(2)}) collective-permute-start(bf16[2,128,1024]{2,1,0:T(8,128)(2,1)S(1)} %get-tuple-element.16), channel_id=1, source_target_pairs={{0,2},{2,0},{1,3},{3,1},{4,6},{6,4},{5,7},{7,5},{8,10},{10,8},{9,1... | collective-permute-start | bytes 1572872 | tf_op jit(solution)/shard_map/ppermute | solution.py:310
  181.0 12.1 %collective-permute-start.20 = (bf16[32,16,128]{2,1,0:T(8,128)(2,1)S(1)}, bf16[32,16,128]{2,1,0:T(8,128)(2,1)S(1)}, u32[]{:S(2)}, u32[]{:S(2)}) collective-permute-start(bf16[32,16,128]{2,1,0:T(8,128)(2,1)S(1)} %get-tuple-element.34), channel_id=1, source_target_pairs={{0,12},{4,8},{8,4},{12,0},{1,13},{5,9},{9,5},{13,1},{2,14},{6,10},... | collective-permute-start | bytes 393224 | tf_op jit(solution)/shard_map/ppermute | solution.py:337
  182.6 11.6 %collective-permute-start.19 = (bf16[32,16,128]{2,1,0:T(8,128)(2,1)S(1)}, bf16[32,16,128]{2,1,0:T(8,128)(2,1)S(1)}, u32[]{:S(2)}, u32[]{:S(2)}) collective-permute-start(bf16[32,16,128]{2,1,0:T(8,128)(2,1)S(1)} %get-tuple-element.35), channel_id=1, source_target_pairs={{0,8},{4,12},{8,0},{12,4},{1,9},{5,13},{9,1},{13,5},{2,10},{6,14},... | collective-permute-start | bytes 393224 | tf_op jit(solution)/shard_map/ppermute | solution.py:337
  183.2 10.9 %collective-permute-start.18 = (bf16[32,16,128]{2,1,0:T(8,128)(2,1)S(1)}, bf16[32,16,128]{2,1,0:T(8,128)(2,1)S(1)}, u32[]{:S(2)}, u32[]{:S(2)}) collective-permute-start(bf16[32,16,128]{2,1,0:T(8,128)(2,1)S(1)} %get-tuple-element.33), channel_id=1, source_target_pairs={{0,4},{4,0},{8,12},{12,8},{1,5},{5,1},{9,13},{13,9},{2,6},{6,2},{1... | collective-permute-start | bytes 393224 | tf_op jit(solution)/shard_map/ppermute | solution.py:337
  189.9 4.2 %copy-start.14 = (f32[1,32,1,128]{3,2,1,0:T(1,128)S(1)}, f32[1,32,1,128]{3,2,1,0:T(1,128)}, u32[]{:S(2)}) copy-start(f32[1,32,1,128]{3,2,1,0:T(1,128)} %get-tuple-element.46) | copy-start | bytes 49156
  189.9 4.2 %copy-start.15 = (f32[1,32,1,128]{3,2,1,0:T(1,128)S(1)}, f32[1,32,1,128]{3,2,1,0:T(1,128)}, u32[]{:S(2)}) copy-start(f32[1,32,1,128]{3,2,1,0:T(1,128)} %get-tuple-element.47) | copy-start | bytes 49156
  189.9 0.8 copy-start.11
Sparse Core Ops, SparseCore 0:
  64.5 23.4 all-gather.1

commit v2 on v1

v2 whole, which is shorter than its diff:
```python
import functools
import math

import jax
import jax.numpy as jnp
from jax import lax
from jax.experimental import pallas as pl
from jax.experimental.pallas import tpu as pltpu
from jax.sharding import PartitionSpec as P

KVH = 4
HD = 128
lowest = -1e30
f32 = jnp.float32
bf16 = jnp.bfloat16
VMEM = 44 << 20
SHORT = pl.CostEstimate(flops=1, bytes_accessed=1, transcendentals=0)


def xor_pairs(axis, bit):
    return [(i, i ^ bit) for i in range(lax.axis_size(axis))]


def after(x, *tokens):
    anywhere = pl.BlockSpec(memory_space=pl.ANY)
    return pl.pallas_call(
        lambda *refs: None,
        in_specs=[anywhere] * (1 + len(tokens)),
        out_specs=anywhere,
        out_shape=jax.ShapeDtypeStruct(x.shape, x.dtype),
        input_output_aliases={0: 0},
        cost_estimate=SHORT,
    )(x, *tokens)


def attention_kernel(limits_ref, place_ref, mine_ref, other_ref, kv_ref, num_ref, stat_ref):
    chips, per_step, rows, _ = mine_ref.shape
    slots = kv_ref.shape[1]
    half = kv_ref.shape[2] // 2
    total = 2 * chips * rows
    step = pl.program_id(0)
    gx, gz = place_ref[0], place_ref[1]
    slot = lax.broadcasted_iota(jnp.int32, (slots, total), 0)
    zero = jnp.zeros((2 * rows, HD), bf16)
    tops, sums = [], []
    for i in range(per_step):
        limit = limits_ref[step * per_step + i]
        wide = []
        for k in range(KVH):
            mine = mine_ref[k ^ gx, i]
            other = other_ref[k ^ gx, i]
            pair = jnp.concatenate(
                [jnp.where(gz == 0, mine, other), jnp.where(gz == 0, other, mine)], axis=0
            )
            wide.append(jnp.concatenate([pair if j == k else zero for j in range(KVH)], axis=1))
        wide = jnp.concatenate(wide, axis=0)
        scores = lax.dot_general(
            kv_ref[i, :, :half], wide, (((1,), (1,)), ((), ())), preferred_element_type=f32
        ) * (1.0 / math.sqrt(HD))
        seen = slot < limit
        scores = jnp.where(seen, scores, lowest)
        top = jnp.max(scores, axis=0, keepdims=True)
        probs = jnp.where(seen, jnp.exp(scores - top), 0.0)
        tops.append(top)
        sums.append(jnp.sum(probs, axis=0, keepdims=True))
        weights = probs.T.astype(bf16)
        full = jnp.dot(weights, kv_ref[i, :, half:], preferred_element_type=f32).astype(bf16)
        for k in range(KVH):
            for z in range(2):
                low = (2 * k + z) * rows
                num_ref[z ^ gz, k ^ gx, i] = full[low : low + rows, k * HD : (k + 1) * HD]
    for n, parts in enumerate((tops, sums)):
        joined = jnp.concatenate(parts, axis=0)
        for k in range(KVH):
            for z in range(2):
                low = (2 * k + z) * rows
                stat_ref[z ^ gz, k ^ gx, n] = joined[:, low : low + rows]


def cached_attention(mine, other, kv_cache, limits, place):
    chips, sequences, rows, _ = mine.shape
    slots, width = kv_cache.shape[1:]
    per_step = 8
    return pl.pallas_call(
        attention_kernel,
        grid_spec=pltpu.PrefetchScalarGridSpec(
            num_scalar_prefetch=2,
            grid=(sequences // per_step,),
            in_specs=[
                pl.BlockSpec((chips, per_step, rows, HD), lambda j, *_: (0, j, 0, 0)),
                pl.BlockSpec((chips, per_step, rows, HD), lambda j, *_: (0, j, 0, 0)),
                pl.BlockSpec((per_step, slots, width), lambda j, *_: (j, 0, 0)),
            ],
            out_specs=[
                pl.BlockSpec((2, chips, per_step, rows, HD), lambda j, *_: (0, 0, j, 0, 0)),
                pl.BlockSpec((2, chips, 2, per_step, rows), lambda j, *_: (0, 0, 0, j, 0)),
            ],
        ),
        out_shape=[
            jax.ShapeDtypeStruct((2, chips, sequences, rows, HD), bf16),
            jax.ShapeDtypeStruct((2, chips, 2, sequences, rows), f32),
        ],
        compiler_params=pltpu.CompilerParams(vmem_limit_bytes=VMEM),
        cost_estimate=SHORT,
    )(limits, place, mine, other, kv_cache)


def thirds(x):
    parts = []
    for _ in range(3):
        parts.append(x.astype(bf16))
        x = x - parts[-1].astype(f32)
    return parts


def pair_kernel(num_ref, other_num_ref, stat_ref, other_stat_ref, out_ref):
    chips, sequences = num_ref.shape[1:3]
    for c in range(chips):
        top = jnp.maximum(stat_ref[0, c, 0], other_stat_ref[c, 0])
        left = jnp.exp(stat_ref[0, c, 0] - top)
        right = jnp.exp(other_stat_ref[c, 0] - top)
        total = stat_ref[0, c, 1] * left + other_stat_ref[c, 1] * right
        parts = thirds(top) + thirds(total)
        parts.append(jnp.zeros((sequences, HD - 6 * parts[0].shape[1]), bf16))
        packed = jnp.concatenate(parts, axis=1)
        rows = out_ref.shape[2]
        for n in range(sequences // rows):
            out_ref[c, sequences + n] = packed[n * rows : (n + 1) * rows]
        left, right = left.T, right.T
        for b in range(sequences):
            out_ref[c, b] = (
                num_ref[0, c, b].astype(f32) * left[:, b : b + 1]
                + other_num_ref[c, b].astype(f32) * right[:, b : b + 1]
            ).astype(bf16)


def join_pair(num, other_num, stat, other_stat):
    first = pl.BlockSpec((1,) + num.shape[1:], lambda j: (0, 0, 0, 0, 0))
    first_stat = pl.BlockSpec((1,) + stat.shape[1:], lambda j: (0, 0, 0, 0, 0))
    rest = pl.BlockSpec(num.shape[1:], lambda j: (0, 0, 0, 0))
    rest_stat = pl.BlockSpec(stat.shape[1:], lambda j: (0, 0, 0, 0))
    _, chips, sequences, rows, _ = num.shape
    out_shape = (chips, sequences + sequences // rows, rows, HD)
    return pl.pallas_call(
        pair_kernel,
        grid=(1,),
        in_specs=[first, rest, first_stat, rest_stat],
        out_specs=pl.BlockSpec(out_shape, lambda j: (0, 0, 0, 0)),
        out_shape=jax.ShapeDtypeStruct(out_shape, bf16),
        compiler_params=pltpu.CompilerParams(vmem_limit_bytes=VMEM),
        cost_estimate=SHORT,
    )(num, other_num, stat, other_stat)


def final_kernel(*refs, count):
    nums = refs[:count]
    q_ref, key_ref, value_ref, out_ref = refs[count:]
    sequences, rows, _ = q_ref.shape
    steps = key_ref.shape[0]
    scale = 1.0 / math.sqrt(HD)
    stats = []
    for r in nums:
        packed = jnp.concatenate([r[b] for b in range(sequences, r.shape[0])], axis=0).astype(f32)
        parts = [packed[:, n * rows : (n + 1) * rows] for n in range(6)]
        stats.append([(sum(parts[n + 1 : n + 3], parts[n])).T for n in (0, 3)])
    step_of = lax.broadcasted_iota(jnp.int32, (rows, 1), 0) // (rows // steps)
    for b in range(sequences):
        q = q_ref[b].astype(f32)
        fresh = []
        for t in range(steps):
            key = key_ref[t, b : b + 1, :].astype(f32)
            score = jnp.sum(q * key, axis=1, keepdims=True) * scale
            fresh.append(jnp.where(step_of >= t, score, lowest))
        tops = [s[0][:, b : b + 1] for s in stats]
        top = functools.reduce(jnp.maximum, tops + fresh)
        num = jnp.zeros((rows, HD), f32)
        den = jnp.zeros((rows, 1), f32)
        for t in range(steps):
            prob = jnp.where(step_of >= t, jnp.exp(fresh[t] - top), 0.0)
            den += prob
            num += prob.astype(bf16).astype(f32) * value_ref[t, b : b + 1, :].astype(f32)
        for n, s, m in zip(nums, stats, tops):
            part = jnp.exp(m - top)
            den += part * s[1][:, b : b + 1]
            num += part * n[b].astype(f32)
        out_ref[b] = (num / den).astype(bf16)


def join_all(nums, q, keys, values):
    return pl.pallas_call(
        functools.partial(final_kernel, count=len(nums)),
        out_shape=jax.ShapeDtypeStruct(q.shape, bf16),
        cost_estimate=SHORT,
    )(*nums, q, keys, values)


def lane_kernel(x_ref, out_ref):
    half = x_ref.shape[1] // 2
    row = lax.broadcasted_iota(jnp.int32, (256, 256), 0)
    col = lax.broadcasted_iota(jnp.int32, (256, 256), 1)
    place = (col == 2 * (row % 128) + row // 128).astype(f32).astype(bf16)
    for c in range(half // 128):
        both = jnp.concatenate(
            [x_ref[:, c * 128 : (c + 1) * 128], x_ref[:, half + c * 128 : half + (c + 1) * 128]],
            axis=1,
        )
        moved = jnp.dot(both, place, preferred_element_type=f32)
        out_ref[:, c * 256 : (c + 1) * 256] = moved.astype(bf16)


def interleave_lanes(x):
    return pl.pallas_call(
        lane_kernel,
        out_shape=jax.ShapeDtypeStruct(x.shape, bf16),
        cost_estimate=SHORT,
    )(x)


def split_rows(first, second):
    rows = first.shape[0]
    odd = (lax.broadcasted_iota(jnp.int32, (1, 8, 128), 1) & 1) == 1
    a = first.astype(f32).reshape(rows // 8, 8, 128)
    b = second.astype(f32).reshape(rows // 8, 8, 128)
    gate = jnp.where(odd, pltpu.roll(b, 1, 1), a)
    up = jnp.where(odd, b, pltpu.roll(a, 7, 1))
    return gate.reshape(rows, 128).astype(bf16), up.reshape(rows, 128).astype(bf16)


def product_kernel(place_ref, *refs, count, cuts, pieces):
    x_ref, sems, x_sems, flat = refs[-4:]
    outs = refs[-4 - len(cuts) : -4]
    left_ref, right_ref = refs[-6 - len(cuts) : -4 - len(cuts)]
    block = x_ref.shape[0] // (2 * len(pieces))
    gz, to_send = place_ref[1], place_ref[2]
    j = pl.program_id(0)
    depth = left_ref.shape[0]
    piece = min(1024, depth)
    halves = [r.reshape(2 * depth, 128) for r in (left_ref, right_ref)]

    def copies(slot):
        return [
            pltpu.make_async_copy(h, flat.at[slot, t], sems.at[slot, t])
            for t, h in enumerate(halves)
        ]

    def fetch(act, chosen):
        for p, sources in enumerate(pieces):
            for core, source in enumerate(sources[chosen]):
                start = pl.multiple_of((2 * p + jnp.bitwise_xor(gz, core)) * block, block)
                act(
                    pltpu.make_async_copy(
                        refs[source], x_ref.at[pl.ds(start, block)], x_sems.at[p, core]
                    )
                )

    @pl.when((j == 0) & (to_send == 1))
    def _():
        fetch(lambda c: c.start(), 0)

    @pl.when((j == 0) & (to_send == 0))
    def _():
        fetch(lambda c: c.start(), 1)

    @pl.when(j < count)
    def _():
        for c in copies(lax.rem(j, 2)):
            c.start()

    @pl.when(j > 0)
    def _():
        slot = lax.rem(j + 1, 2)
        rows = x_ref.shape[0]
        gate = up = jnp.zeros((rows, 256), f32)
        for i in range(0, depth, piece):
            sides = [
                split_rows(flat[slot, t, i : i + piece], flat[slot, t, depth + i : depth + i + piece])
                for t in range(2)
            ]
            x = x_ref[:, i : i + piece]
            gate += jnp.dot(
                x, jnp.concatenate([s[0] for s in sides], 1), preferred_element_type=f32
            )
            up += jnp.dot(x, jnp.concatenate([s[1] for s in sides], 1), preferred_element_type=f32)
        low = 0
        for ref, high in zip(outs, cuts):
            ref[0] = gate[low:high].astype(bf16)
            ref[1] = up[low:high].astype(bf16)
            low = high

    @pl.when(j < count)
    def _():
        for c in copies(lax.rem(j, 2)):
            c.wait()

    @pl.when(j == 0)
    def _():
        fetch(lambda c: c.wait(), 0)


def product(place, blocks, pieces, weights, first, last, cuts, *tokens):
    block, depth = blocks[0].shape
    rows = 2 * len(pieces) * block
    count = last - first
    sizes = [high - low for low, high in zip((0,) + cuts[:-1], cuts)]
    anywhere = [pl.BlockSpec(memory_space=pl.ANY)]
    stay = [pl.BlockSpec(memory_space=pltpu.HBM)]

    def column(side):
        return pl.BlockSpec(
            (depth, 1, 2, 128),
            lambda j, _: (0, 2 * (first + jnp.minimum(j, count - 1)) + side, 0, 0),
        )

    return pl.pallas_call(
        functools.partial(product_kernel, count=count, cuts=cuts, pieces=pieces),
        grid_spec=pltpu.PrefetchScalarGridSpec(
            num_scalar_prefetch=1,
            grid=(count + 1,),
            in_specs=anywhere * len(blocks) + stay * len(tokens) + [column(0), column(1)],
            out_specs=[
                pl.BlockSpec((2, size, 256), lambda j, _: (0, 0, jnp.maximum(j - 1, 0)))
                for size in sizes
            ],
            scratch_shapes=[
                pltpu.VMEM((rows, depth), bf16),
                pltpu.SemaphoreType.DMA((2, 2)),
                pltpu.SemaphoreType.DMA((len(pieces), 2)),
                pltpu.VMEM((2, 2, 2 * depth, 128), bf16),
            ],
        ),
        out_shape=[jax.ShapeDtypeStruct((2, size, count * 256), bf16) for size in sizes],
        compiler_params=pltpu.CompilerParams(vmem_limit_bytes=VMEM),
        cost_estimate=SHORT,
    )(place, *blocks, *tokens, weights, weights)


def gated_kernel(swap_ref, held_ref, kept_ref, near_ref, far_ref, out_ref):
    half = near_ref.shape[1]
    for i, theirs in enumerate((near_ref, far_ref)):
        rows = slice(i * half, (i + 1) * half)
        gate = kept_ref[0, rows].astype(f32) + theirs[0].astype(f32)
        up = kept_ref[1, rows].astype(f32) + theirs[1].astype(f32)
        start = jnp.bitwise_xor(swap_ref[0], i) * half
        out_ref[pl.ds(pl.multiple_of(start, half), half), :] = (jax.nn.silu(gate) * up).astype(bf16)


def gated(kept, near, far, swap, held, first, width):
    rows, half, columns = kept.shape[1], near.shape[1], kept.shape[2]
    wide = 512 if columns % 512 == 0 and first % 2 == 0 else 256
    return pl.pallas_call(
        gated_kernel,
        grid_spec=pltpu.PrefetchScalarGridSpec(
            num_scalar_prefetch=1,
            grid=(columns // wide,),
            in_specs=[
                pl.BlockSpec(memory_space=pl.ANY),
                pl.BlockSpec((2, rows, wide), lambda j, _: (0, 0, j)),
                pl.BlockSpec((2, half, wide), lambda j, _: (0, 0, j)),
                pl.BlockSpec((2, half, wide), lambda j, _: (0, 0, j)),
            ],
            out_specs=pl.BlockSpec((rows, wide), lambda j, _: (0, first * 256 // wide + j)),
        ),
        out_shape=jax.ShapeDtypeStruct((rows, width), bf16),
        input_output_aliases={} if held is None else {1: 0},
        cost_estimate=SHORT,
    )(swap, kept if held is None else held, kept, near, far)


def on_device(prompt_rows, gate_up, queries, new_kv, kv_cache, lengths):
    gx, gy, gz = (lax.axis_index(a) for a in ("gx", "gy", "gz"))
    chips = lax.axis_size("gx")
    cores = lax.axis_size("gz")
    depth, _, width = gate_up.shape
    block = prompt_rows.shape[0]
    to_send = ((gx // 2) != gy).astype(jnp.int32)
    place = jnp.stack([gx, gz, to_send])
    over = [(0, 1), (1, 0)]

    mine = interleave_lanes(prompt_rows)
    along = lax.ppermute(mine, "gx", xor_pairs("gx", 2))
    mine_far = lax.ppermute(mine, "gx", xor_pairs("gx", 1))
    mine_other = lax.ppermute(mine, "gz", over)

    steps = queries.shape[0]
    sequences, slots = kv_cache.shape[:2]
    me = gx * cores + gz
    heads = queries.shape[2] // HD
    rows = steps * heads
    my_q = queries.reshape(steps, sequences, heads, HD).transpose(1, 0, 2, 3)
    my_q = after(my_q.reshape(1, sequences, rows, HD), mine)
    all_q = jnp.concatenate(
        [my_q] + [lax.ppermute(my_q, "gx", xor_pairs("gx", bit)) for bit in range(1, chips)], axis=0
    )
    other_q = lax.ppermute(all_q, "gz", over)
    limits = jnp.clip(lengths - me * slots, 0, slots)
    num, stat = cached_attention(all_q, other_q, kv_cache, limits, place)

    along = after(along, num)
    along_other = lax.ppermute(along, "gz", over)
    along_far = lax.ppermute(along, "gx", xor_pairs("gx", 1))
    mine_far_other = lax.ppermute(mine_far, "gz", over)
    along_far_other = lax.ppermute(along_far, "gz", over)

    other_num = lax.ppermute(num[1], "gz", over)
    other_stat = lax.ppermute(stat[1], "gz", over)
    pair = join_pair(num, other_num, stat, other_stat)
    nums = [pair[0]]
    for bit in range(1, chips):
        nums.append(lax.ppermute(pair[bit], "gx", xor_pairs("gx", bit)))
    units = new_kv.reshape(steps, sequences, 2 * KVH, HD)
    keys = lax.dynamic_index_in_dim(units, gx, 2, False)
    values = lax.dynamic_index_in_dim(units, gx + KVH, 2, False)
    attended = join_all(nums, my_q[0], keys, values)

    weights = gate_up.reshape(depth, 2, width // 128, 128).transpose(0, 2, 1, 3)
    pairs = width // 256
    cuts = [0, pairs // 14 * 4, pairs // 14 * 10, pairs] if pairs % 14 == 0 else [0, pairs]
    spans = list(zip(cuts[:-1], cuts[1:]))
    half = cores * block
    swap = (gx % 2).reshape(1)
    near, tokens = [], (num,)
    blocks = (mine, mine_other, along, along_other)
    pieces = (((0, 1), (2, 3)),)
    for i, (first, last) in enumerate(spans):
        (out,) = product(place, blocks, pieces, weights, first, last, (half,), *tokens)
        near.append(lax.ppermute(out, "gy", over))
        tokens = (out, pair)
    blocks += (mine_far, mine_far_other, along_far, along_far_other)
    pieces = (((4, 5), (6, 7)), ((2, 3), (0, 1)), ((6, 7), (4, 5)))
    tokens = (out, near[0])
    hidden_units = None
    waiting = []
    for i, (first, last) in enumerate(spans):
        sent, keep = product(place, blocks, pieces, weights, first, last, (half, 3 * half), *tokens)
        waiting.append((keep, near[i], lax.ppermute(sent, "gy", over), first))
        tokens = (keep, near[min(i + 1, len(near) - 1)], *nums[1:])
        if i + 1 >= len(spans) - 1 and len(waiting) > 1:
            keep, early, late, start = waiting.pop(0)
            hidden_units = gated(keep, early, late, swap, hidden_units, start, width)
            tokens += (hidden_units,)
    for keep, early, late, start in waiting:
        hidden_units = gated(keep, early, late, swap, hidden_units, start, width)

    attended = attended.reshape(sequences, steps, heads, HD).transpose(1, 0, 2, 3)
    return hidden_units, attended.reshape(steps, sequences, heads * HD)


def plain_on_device(prompt_rows, gate_up, queries, new_kv, kv_cache, lengths):
    partial_terms = jnp.dot(
        lax.all_gather(prompt_rows, ("gx", "gz"), axis=0, tiled=True),
        gate_up.reshape(gate_up.shape[0], -1),
        preferred_element_type=f32,
    )
    summed = lax.psum_scatter(
        partial_terms.astype(bf16), "gy", scatter_dimension=0, tiled=True
    ).astype(f32)
    summed = summed.reshape(summed.shape[0], 2, -1)
    hidden_units = (jax.nn.silu(summed[:, 0]) * summed[:, 1]).astype(bf16)
    members = lax.axis_size(("gx", "gz"))
    me = lax.axis_index(("gx", "gz"))
    steps = queries.shape[0]
    sequences, slots = kv_cache.shape[:2]
    all_q = lax.all_gather(queries, ("gx", "gz"), axis=2, tiled=True)
    grouped = all_q.reshape(steps, sequences, KVH, -1, HD)
    cache = kv_cache.reshape(sequences, slots, 2, KVH, HD)
    fresh = new_kv.reshape(steps, sequences, 2, KVH, HD).transpose(1, 0, 2, 3, 4)
    units = jnp.concatenate([cache, fresh], axis=1)
    scores = jnp.einsum(
        "sukgd,ujkd->sukgj", grouped, units[:, :, 0], preferred_element_type=f32
    ) * (1.0 / math.sqrt(HD))
    cached = me * slots + jnp.arange(slots, dtype=jnp.int32)[None, :] < lengths[:, None]
    ids = jnp.arange(steps, dtype=jnp.int32)
    fresh_seen = (ids[None, :] <= ids[:, None]) & (me == 0)
    seen = jnp.concatenate(
        [
            jnp.broadcast_to(cached[None], (steps, sequences, slots)),
            jnp.broadcast_to(fresh_seen[:, None, :], (steps, sequences, steps)),
        ],
        axis=2,
    )[:, :, None, None, :]
    masked = jnp.where(seen, scores, lowest)
    top = jnp.max(masked, axis=-1)
    probs = jnp.where(seen, jnp.exp(masked - top[..., None]), 0.0)
    den = jnp.sum(probs, axis=-1)
    num = jnp.einsum(
        "sukgj,ujkd->sukgd", probs.astype(bf16), units[:, :, 1], preferred_element_type=f32
    )
    overall = lax.pmax(top, ("gx", "gz"))
    scale = jnp.exp(top - overall)
    num = (num * scale[..., None]).reshape(steps, sequences, -1, HD)
    den = (den * scale).reshape(steps, sequences, -1)
    num = lax.psum_scatter(
        num.astype(bf16), ("gx", "gz"), scatter_dimension=2, tiled=True
    ).astype(f32)
    den = lax.psum_scatter(den, ("gx", "gz"), scatter_dimension=2, tiled=True)
    attended = (num / den[..., None]).astype(bf16)
    return hidden_units, attended.reshape(steps, sequences, -1)


def solution(mesh):
    sizes = mesh.shape
    paired = sizes["gy"] == 2 and sizes["gx"] == KVH and sizes["gz"] == 2
    return jax.shard_map(
        on_device if paired else plain_on_device,
        mesh=mesh,
        in_specs=(
            P(("groups", "gx", "gz"), "gy"),
            P("gy", None, ("gx", "gz")),
            P(None, ("groups", "gy"), ("gx", "gz")),
            P(None, ("groups", "gy"), None),
            P(("groups", "gy"), ("gx", "gz"), None),
            P(("groups", "gy")),
        ),
        out_specs=(P(("groups", "gy"), ("gx", "gz")), P(None, ("groups", "gy"), ("gx", "gz"))),
        check_vma=False,
    )
```

time: 203 us -> 180 us (0.89)
  between operations: 16.5 us -> 1.01 us
  waiting for transfers between devices: 33.3 us -> 22.9 us
  Pallas kernels: 108 us -> 117 us
  other arithmetic: 9.82 us -> 1.05 us
  local copies, waits for them, and re-layouts: 12.1 us -> 17.7 us
    ppermute x18 -> x19, waiting for transfers between devices: 33.3 us -> 22.9 us  [the longest x3 10.7 us: on_device(): lax.ppermute(my_q, 'gx', xor_pairs('gx', bit))]
    pallas_call x7 -> x11, Pallas kernels: 97.6 us -> 106 us  [the longest x6 81.6 us: product(): pl.pallas_call(functools.partial(product_kernel, count=count, cuts=cuts,...]
    unnamed x37 -> x54, local copies, waits for them, and re-layouts: 7.92 us -> 13.9 us
    unnamed x5 -> x0, other arithmetic: 4.83 us -> none
    ppermute x18 -> x19, starting transfers between devices: 18.4 us -> 17.5 us  [the longest x3 5.62 us: on_device(): lax.ppermute(my_q, 'gx', xor_pairs('gx', bit))]
  transfers between devices with their start and end apart: 22 -> 22, of which waited for: 5 -> 6; matrix products, arithmetic and copies ran while one was open for 6% -> 2% of each run, Pallas kernels for 52% -> 62%
where the time goes in v2:
time: 180 us; the launch traced here: 179 us
  Pallas kernels  117 us (65%)
  waiting for transfers between devices  22.9 us (13%)
  starting transfers between devices  20.2 us (11%)
  local copies, waits for them, and re-layouts  17.7 us (10%)
    pallas_call x6, Pallas kernels, product(): pl.pallas_call(functools.partial(product_kernel, count=count, cuts=cuts,...  81.6 us
    pallas_call x1, Pallas kernels, cached_attention(): pl.pallas_call(attention_kernel, grid_spec=pltpu.PrefetchScalarGridSpec(n...  17.1 us
    unnamed x54, local copies, waits for them, and re-layouts  13.9 us
    ppermute x3, waiting for transfers between devices, on_device(): lax.ppermute(my_q, 'gx', xor_pairs('gx', bit))  10.7 us
    pallas_call x3, Pallas kernels, gated(): pl.pallas_call(gated_kernel, grid_spec=pltpu.PrefetchScalarGridSpec(num_s...  8.58 us
    ppermute x3, waiting for transfers between devices, on_device(): nums.append(lax.ppermute(pair[bit], 'gx', xor_pairs('gx', bit)))  6.1 us
    pallas_call x1, Pallas kernels, join_all(): pl.pallas_call(functools.partial(final_kernel, count=len(nums)), out_shap...  6.06 us
    ppermute x3, starting transfers between devices, on_device(): lax.ppermute(my_q, 'gx', xor_pairs('gx', bit))  5.62 us
  transfers between devices with their start and end apart: 22, of which 6 were waited for; matrix products, arithmetic and copies ran while one was open for 2% of the time, Pallas kernels for 62%

profile of v2, /device:TPU:0, one launch (start us, length us, event | category | flops | bytes accessed | tf_op | source)
XLA Modules:
  0.0 179.3 jit_solution(2862485956643747721)
XLA Ops:
  0.6 0.9 copy.19
  1.6 0.7 copy_bitcast_fusion.refs_0_
  2.3 2.3 %shard_map.77.refs_1_.refs_0_ = bf16[64,4096]{1,0:T(8,128)(2,1)} custom-call(bf16[64,4096]{1,0:T(8,128)(2,1)} %x_ref.1), custom_call_target="tpu_custom_call" | custom-call | flops 1 | bytes 1 | tf_op jit(solution)/shard_map/pallas_call | solution.py:212
  4.6 5.0 %collective-permute-start.4 = (bf16[1,32,16,128]{3,2,1,0:T(8,128)(2,1)}, bf16[1,32,16,128]{3,2,1,0:T(8,128)(2,1)S(1)}, u32[]{:S(2)}, u32[]{:S(2)}) collective-permute-start(bf16[1,32,16,128]{3,2,1,0:T(8,128)(2,1)} %shard_map.78), channel_id=1, source_target_pairs={{0,12},{4,8},{8,4},{12,0},{1,13},{5,9},{9,5},{13,1},{2,14},{6,10},... | collective-permute-start | bytes 393224 | tf_op jit(solution)/shard_map/ppermute | solution.py:392
  9.6 0.6 collective-permute-start.2
  10.2 4.1 %collective-permute-done.4 = bf16[1,32,16,128]{3,2,1,0:T(8,128)(2,1)S(1)} collective-permute-done((bf16[1,32,16,128]{3,2,1,0:T(8,128)(2,1)}, bf16[1,32,16,128]{3,2,1,0:T(8,128)(2,1)S(1)}, u32[]{:S(2)}, u32[]{:S(2)}) %collective-permute-start.4) | collective-permute-done | bytes 131104 | tf_op jit(solution)/shard_map/ppermute | solution.py:392
  14.3 6.6 %collective-permute-done.3 = bf16[1,32,16,128]{3,2,1,0:T(8,128)(2,1)S(1)} collective-permute-done((bf16[1,32,16,128]{3,2,1,0:T(8,128)(2,1)}, bf16[1,32,16,128]{3,2,1,0:T(8,128)(2,1)S(1)}, u32[]{:S(2)}, u32[]{:S(2)}) %collective-permute-start.3) | collective-permute-done | bytes 131104 | tf_op jit(solution)/shard_map/ppermute | solution.py:392
  20.9 1.0 pad_maximum_fusion.mine_ref
  22.1 3.0 %collective-permute-start.7 = (bf16[64,4096]{1,0:T(8,128)(2,1)}, bf16[64,4096]{1,0:T(8,128)(2,1)}, u32[]{:S(2)}, u32[]{:S(2)}) collective-permute-start(bf16[64,4096]{1,0:T(8,128)(2,1)} %shard_map.77.refs_1_.refs_0_), channel_id=1, source_target_pairs={{0,4},{4,0},{8,12},{12,8},{1,5},{5,1},{9,13},{13,9},{2,6},{6,2},{1... | collective-permute-start | bytes 1572872 | tf_op jit(solution)/shard_map/ppermute | solution.py:381
  25.2 17.1 %shard_map.79 = (bf16[2,4,32,16,128]{4,3,2,1,0:T(8,128)(2,1)S(1)}, f32[2,4,2,32,16]{4,3,2,1,0:T(8,128)S(1)}) custom-call(s32[32]{0:T(128)S(1)} %subtract_clamp_fusion.limits_ref, s32[3]{0:T(128)S(1)} %pad_add_fusion.place_ref, bf16[4,32,16,128]{3,2,1,0:T(8,128)(2,1)S(1)} %pad_maximum_fusion.mine_ref, ...), custom_call_target="tpu_custom_call" | custom-call | flops 1 | bytes 1 | tf_op jit(solution)/shard_map/pallas_call | solution.py:84
  42.3 1.0 copy-done.5
  43.2 5.3 %collective-permute-done.1.refs_0_ = bf16[64,4096]{1,0:T(8,128)(2,1)S(1)} collective-permute-done((bf16[64,4096]{1,0:T(8,128)(2,1)}, bf16[64,4096]{1,0:T(8,128)(2,1)S(1)}, u32[]{:S(2)}, u32[]{:S(2)}) %collective-permute-start.1) | collective-permute-done | bytes 524320 | tf_op jit(solution)/shard_map/ppermute | solution.py:380
  48.6 0.8 copy-done.2
  49.4 0.6 copy-done.6
  50.8 0.7 collective-permute-done.6.refs_3_
  51.5 1.0 copy-done.3
  52.6 10.5 %shard_map.81.refs_4_ = bf16[2,128,1024]{2,1,0:T(8,128)(2,1)S(1)} custom-call(s32[3]{0:T(128)S(1)} %pad_add_fusion.place_ref, bf16[64,4096]{1,0:T(8,128)(2,1)S(1)} %copy-done, bf16[64,4096]{1,0:T(8,128)(2,1)S(1)} %collective-permute-done.refs_1_, bf16[64,4096]{1,0:T(8,128)(2,1)S(1)} %copy-done.3, bf16[64,4096]{1,0:T(8,128)(2,1)S(1)} %collective-permute-done.6.refs_3_, ...), custom_call_target="tpu_custom_call" | custom-call | flops 1 | bytes 1 | tf_op jit(solution)/shard_map/pallas_call | solution.py:314
  63.1 1.6 collective-permute-start.13
  64.7 0.9 shard_map.82.refs_5_
  65.6 14.3 %shard_map.83.refs_4_ = bf16[2,128,1536]{2,1,0:T(8,128)(2,1)S(1)} custom-call(s32[3]{0:T(128)S(1)} %pad_add_fusion.place_ref, bf16[64,4096]{1,0:T(8,128)(2,1)S(1)} %copy-done, bf16[64,4096]{1,0:T(8,128)(2,1)S(1)} %collective-permute-done.refs_1_, bf16[64,4096]{1,0:T(8,128)(2,1)S(1)} %copy-done.4, bf16[64,4096]{1,0:T(8,128)(2,1)S(1)} %collective-permute-done.6.refs_3_, ...), custom_call_target="tpu_custom_call" | custom-call | flops 1 | bytes 1 | tf_op jit(solution)/shard_map/pallas_call | solution.py:314
  79.9 0.6 collective-permute-start.15
  80.5 0.7 slice_bitcast_fusion.1
  81.3 1.3 collective-permute-start.18
  82.6 11.2 %shard_map.84.refs_8_ = bf16[2,128,1024]{2,1,0:T(8,128)(2,1)} custom-call(s32[3]{0:T(128)S(1)} %pad_add_fusion.place_ref, bf16[64,4096]{1,0:T(8,128)(2,1)S(1)} %copy-done, bf16[64,4096]{1,0:T(8,128)(2,1)S(1)} %collective-permute-done.refs_1_, bf16[64,4096]{1,0:T(8,128)(2,1)S(1)} %copy-done.4, bf16[64,4096]{1,0:T(8,128)(2,1)S(1)} %collective-permute-done.6.refs_3_, ...), custom_call_target="tpu_custom_call" | custom-call | flops 1 | bytes 1 | tf_op jit(solution)/shard_map/pallas_call | solution.py:314
  93.9 13.6 %shard_map.85 = (bf16[2,128,1024]{2,1,0:T(8,128)(2,1)}, bf16[2,256,1024]{2,1,0:T(8,128)(2,1)S(1)}) custom-call(s32[3]{0:T(128)S(1)} %pad_add_fusion.place_ref, bf16[64,4096]{1,0:T(8,128)(2,1)S(1)} %copy-done, bf16[64,4096]{1,0:T(8,128)(2,1)S(1)} %collective-permute-done.refs_1_, bf16[64,4096]{1,0:T(8,128)(2,1)S(1)} %copy-done.4, ...), custom_call_target="tpu_custom_call" | custom-call | flops 1 | bytes 1 | tf_op jit(solution)/shard_map/pallas_call | solution.py:314
  107.5 1.6 collective-permute-start.14
  109.6 2.1 %collective-permute-start.17 = (bf16[34,16,128]{2,1,0:T(8,128)(2,1)S(1)}, bf16[34,16,128]{2,1,0:T(8,128)(2,1)S(1)}, u32[]{:S(2)}, u32[]{:S(2)}) collective-permute-start(bf16[34,16,128]{2,1,0:T(8,128)(2,1)S(1)} %get-tuple-element.20), channel_id=1, source_target_pairs={{0,8},{4,12},{8,0},{12,4},{1,9},{5,13},{9,1},{13,5},{2,10},{6,14},... | collective-permute-start | bytes 417800 | tf_op jit(solution)/shard_map/ppermute | solution.py:409
  111.8 0.9 collective-permute-start.16
  112.7 5.9 %collective-permute-done.17.refs_11_.refs_2_ = bf16[34,16,128]{2,1,0:T(8,128)(2,1)S(1)} collective-permute-done((bf16[34,16,128]{2,1,0:T(8,128)(2,1)S(1)}, bf16[34,16,128]{2,1,0:T(8,128)(2,1)S(1)}, u32[]{:S(2)}, u32[]{:S(2)}) %collective-permute-start.17) | collective-permute-done | bytes 139296 | tf_op jit(solution)/shard_map/ppermute | solution.py:409
  118.8 18.3 %shard_map.87 = (bf16[2,128,1536]{2,1,0:T(8,128)(2,1)}, bf16[2,256,1536]{2,1,0:T(8,128)(2,1)S(1)}) custom-call(s32[3]{0:T(128)S(1)} %pad_add_fusion.place_ref, bf16[64,4096]{1,0:T(8,128)(2,1)S(1)} %copy-done, bf16[64,4096]{1,0:T(8,128)(2,1)S(1)} %collective-permute-done.refs_1_, bf16[64,4096]{1,0:T(8,128)(2,1)S(1)} %copy-done.4, ...), custom_call_target="tpu_custom_call" | custom-call | flops 1 | bytes 1 | tf_op jit(solution)/shard_map/pallas_call | solution.py:314
  137.1 1.2 copy-done.8
  138.3 1.5 collective-permute-start.19
  139.8 0.8 copy-done.24
  140.6 2.5 %shard_map.86.held_ref.refs_13_ = bf16[256,3584]{1,0:T(8,128)(2,1)} custom-call(s32[1]{0:T(128)} %bitcast.swap_ref, bf16[2,256,1024]{2,1,0:T(8,128)(2,1)} %copy-done.7, bf16[2,256,1024]{2,1,0:T(8,128)(2,1)} %copy-done.7, bf16[2,128,1024]{2,1,0:T(8,128)(2,1)} %copy-done.17, bf16[2,128,1024]{2,1,0:T(8,128)(2,1)} %copy-done.24), custom_call_target="tpu_custom_call" | custom-call | flops 1 | bytes 1 | tf_op jit(solution)/shard_map/pallas_call | solution.py:350
  143.1 1.5 copy-done.1
  144.6 1.4 copy-done.9
  146.0 1.0 copy-done.15
  147.0 0.9 copy-done.21
  147.9 13.6 %shard_map.89 = (bf16[2,128,1024]{2,1,0:T(8,128)(2,1)}, bf16[2,256,1024]{2,1,0:T(8,128)(2,1)S(1)}) custom-call(s32[3]{0:T(128)S(1)} %pad_add_fusion.place_ref, bf16[64,4096]{1,0:T(8,128)(2,1)S(1)} %copy-done, bf16[64,4096]{1,0:T(8,128)(2,1)S(1)} %collective-permute-done.refs_1_, bf16[64,4096]{1,0:T(8,128)(2,1)S(1)} %copy-done.4, ...), custom_call_target="tpu_custom_call" | custom-call | flops 1 | bytes 1 | tf_op jit(solution)/shard_map/pallas_call | solution.py:314
  161.6 1.0 copy-done.22
  163.1 0.9 copy.20
  164.1 0.6 copy_bitcast_fusion.1
  164.7 6.1 %shard_map.91 = bf16[32,16,128]{2,1,0:T(8,128)(2,1)} custom-call(bf16[34,16,128]{2,1,0:T(8,128)(2,1)} %get-tuple-element.18.refs_0_, bf16[34,16,128]{2,1,0:T(8,128)(2,1)} %copy-done.20, bf16[34,16,128]{2,1,0:T(8,128)(2,1)} %copy-done.19, bf16[34,16,128]{2,1,0:T(8,128)(2,1)} %copy-done.18, bf16[32,16,128]{2,1,0:T(8,128)(2,1)} %bitcast.59, ...), custom_call_target="tpu_custom_call" | custom-call | flops 1 | bytes 1 | tf_op jit(solution)/shard_map/pallas_call | solution.py:190
  170.8 0.9 reshape.33
  171.7 0.7 copy.16
  172.4 3.7 %shard_map.88.held_ref = bf16[256,3584]{1,0:T(8,128)(2,1)} custom-call(s32[1]{0:T(128)} %bitcast.swap_ref, bf16[256,3584]{1,0:T(8,128)(2,1)} %shard_map.86.held_ref.refs_13_, bf16[2,256,1536]{2,1,0:T(8,128)(2,1)} %copy-done.8, bf16[2,128,1536]{2,1,0:T(8,128)(2,1)} %copy-done.16, ...), custom_call_target="tpu_custom_call", output_to_operand_aliasing={{}: (1, {})} | custom-call | flops 1 | bytes 1 | tf_op jit(solution)/shard_map/pallas_call | solution.py:350
  176.1 0.8 copy-done.23
  176.9 2.4 %shard_map.90 = bf16[256,3584]{1,0:T(8,128)(2,1)} custom-call(s32[1]{0:T(128)} %bitcast.swap_ref, bf16[256,3584]{1,0:T(8,128)(2,1)} %shard_map.88.held_ref, bf16[2,256,1024]{2,1,0:T(8,128)(2,1)} %copy-done.22, bf16[2,128,1024]{2,1,0:T(8,128)(2,1)} %collective-permute-done.20.refs_9_.near_ref, ...), custom_call_target="tpu_custom_call", output_to_operand_aliasing={{}: (1, {})} | custom-call | flops 1 | bytes 1 | tf_op jit(solution)/shard_map/pallas_call | solution.py:350
  (76 shorter events, 2.5 us)
Async XLA Ops:
  0.6 24.5 %copy-start.25 = (s32[32]{0:T(128)S(1)}, s32[32]{0:T(128)}, u32[]{:S(2)}) copy-start(s32[32]{0:T(128)} %param.11) | copy-start | bytes 388
  4.6 9.7 %collective-permute-start.4 = (bf16[1,32,16,128]{3,2,1,0:T(8,128)(2,1)}, bf16[1,32,16,128]{3,2,1,0:T(8,128)(2,1)S(1)}, u32[]{:S(2)}, u32[]{:S(2)}) collective-permute-start(bf16[1,32,16,128]{3,2,1,0:T(8,128)(2,1)} %shard_map.78), channel_id=1, source_target_pairs={{0,12},{4,8},{8,4},{12,0},{1,13},{5,9},{9,5},{13,1},{2,14},{6,10},... | collective-permute-start | bytes 393224 | tf_op jit(solution)/shard_map/ppermute | solution.py:392
  9.6 11.3 %collective-permute-start.3 = (bf16[1,32,16,128]{3,2,1,0:T(8,128)(2,1)}, bf16[1,32,16,128]{3,2,1,0:T(8,128)(2,1)S(1)}, u32[]{:S(2)}, u32[]{:S(2)}) collective-permute-start(bf16[1,32,16,128]{3,2,1,0:T(8,128)(2,1)} %shard_map.78), channel_id=1, source_target_pairs={{0,8},{4,12},{8,0},{12,4},{1,9},{5,13},{9,1},{13,5},{2,10},{6,14},... | collective-permute-start | bytes 393224 | tf_op jit(solution)/shard_map/ppermute | solution.py:392
  9.6 11.3 %collective-permute-start.2 = (bf16[1,32,16,128]{3,2,1,0:T(8,128)(2,1)}, bf16[1,32,16,128]{3,2,1,0:T(8,128)(2,1)S(1)}, u32[]{:S(2)}, u32[]{:S(2)}) collective-permute-start(bf16[1,32,16,128]{3,2,1,0:T(8,128)(2,1)} %shard_map.78), channel_id=1, source_target_pairs={{0,4},{4,0},{8,12},{12,8},{1,5},{5,1},{9,13},{13,9},{2,6},{6,2},{1... | collective-permute-start | bytes 393224 | tf_op jit(solution)/shard_map/ppermute | solution.py:392
  21.9 3.3 %collective-permute-start.5 = (bf16[4,32,16,128]{3,2,1,0:T(8,128)(2,1)S(1)}, bf16[4,32,16,128]{3,2,1,0:T(8,128)(2,1)S(1)}, u32[]{:S(2)}, u32[]{:S(2)}) collective-permute-start(bf16[4,32,16,128]{3,2,1,0:T(8,128)(2,1)S(1)} %pad_maximum_fusion.mine_ref), channel_id=1, source_target_pairs={{0,1},{1,0},{2,3},{3,2},{4,5},{5,4},{6,7},{7,6},{8,9},{9,8},{10,11... | collective-permute-start | bytes 1572872 | tf_op jit(solution)/shard_map/ppermute | solution.py:394
  22.0 26.6 %collective-permute-start.1 = (bf16[64,4096]{1,0:T(8,128)(2,1)}, bf16[64,4096]{1,0:T(8,128)(2,1)S(1)}, u32[]{:S(2)}, u32[]{:S(2)}) collective-permute-start(bf16[64,4096]{1,0:T(8,128)(2,1)} %shard_map.77.refs_1_.refs_0_), channel_id=1, source_target_pairs={{0,8},{4,12},{8,0},{12,4},{1,9},{5,13},{9,1},{13,5},{2,10},{6,14},... | collective-permute-start | bytes 1572872 | tf_op jit(solution)/shard_map/ppermute | solution.py:380
  22.1 28.1 %collective-permute-start.7 = (bf16[64,4096]{1,0:T(8,128)(2,1)}, bf16[64,4096]{1,0:T(8,128)(2,1)}, u32[]{:S(2)}, u32[]{:S(2)}) collective-permute-start(bf16[64,4096]{1,0:T(8,128)(2,1)} %shard_map.77.refs_1_.refs_0_), channel_id=1, source_target_pairs={{0,4},{4,0},{8,12},{12,8},{1,5},{5,1},{9,13},{13,9},{2,6},{6,2},{1... | collective-permute-start | bytes 1572872 | tf_op jit(solution)/shard_map/ppermute | solution.py:381
  25.1 25.6 %collective-permute-start = (bf16[64,4096]{1,0:T(8,128)(2,1)}, bf16[64,4096]{1,0:T(8,128)(2,1)S(1)}, u32[]{:S(2)}, u32[]{:S(2)}) collective-permute-start(bf16[64,4096]{1,0:T(8,128)(2,1)} %shard_map.77.refs_1_.refs_0_), channel_id=1, source_target_pairs={{0,1},{1,0},{2,3},{3,2},{4,5},{5,4},{6,7},{7,6},{8,9},{9,8},{10,11... | collective-permute-start | bytes 1572872 | tf_op jit(solution)/shard_map/ppermute | solution.py:382
  42.3 1.0 copy-start.5
  43.2 8.3 %copy-start = (bf16[64,4096]{1,0:T(8,128)(2,1)S(1)}, bf16[64,4096]{1,0:T(8,128)(2,1)}, u32[]{:S(2)}) copy-start(bf16[64,4096]{1,0:T(8,128)(2,1)} %shard_map.77.refs_1_.refs_0_) | copy-start | bytes 1572868
  48.6 0.8 copy-start.2
  48.6 1.4 copy-start.6
  49.4 15.3 %collective-permute-start.9 = (bf16[64,4096]{1,0:T(8,128)(2,1)}, bf16[64,4096]{1,0:T(8,128)(2,1)S(1)}, u32[]{:S(2)}, u32[]{:S(2)}) collective-permute-start(bf16[64,4096]{1,0:T(8,128)(2,1)} %shard_map.80.refs_2_), channel_id=1, source_target_pairs={{0,4},{4,0},{8,12},{12,8},{1,5},{5,1},{9,13},{13,9},{2,6},{6,2},{1... | collective-permute-start | bytes 1572872 | tf_op jit(solution)/shard_map/ppermute | solution.py:400
  49.4 2.1 %collective-permute-start.6 = (bf16[64,4096]{1,0:T(8,128)(2,1)}, bf16[64,4096]{1,0:T(8,128)(2,1)S(1)}, u32[]{:S(2)}, u32[]{:S(2)}) collective-permute-start(bf16[64,4096]{1,0:T(8,128)(2,1)} %shard_map.80.refs_2_), channel_id=1, source_target_pairs={{0,1},{1,0},{2,3},{3,2},{4,5},{5,4},{6,7},{7,6},{8,9},{9,8},{10,11... | collective-permute-start | bytes 1572872 | tf_op jit(solution)/shard_map/ppermute | solution.py:399
  50.0 14.6 %collective-permute-start.11 = (bf16[4,32,16,128]{3,2,1,0:T(8,128)(2,1)S(1)}, bf16[4,32,16,128]{3,2,1,0:T(8,128)(2,1)S(1)}, u32[]{:S(2)}, u32[]{:S(2)}) collective-permute-start(bf16[4,32,16,128]{3,2,1,0:T(8,128)(2,1)S(1)} %slice_bitcast_fusion), channel_id=1, source_target_pairs={{0,1},{1,0},{2,3},{3,2},{4,5},{5,4},{6,7},{7,6},{8,9},{9,8},{10,11... | collective-permute-start | bytes 1572872 | tf_op jit(solution)/shard_map/ppermute | solution.py:404
  50.1 14.5 %collective-permute-start.12 = (f32[4,2,32,16]{3,2,1,0:T(8,128)S(1)}, f32[4,2,32,16]{3,2,1,0:T(8,128)S(1)}, u32[]{:S(2)}, u32[]{:S(2)}) collective-permute-start(f32[4,2,32,16]{3,2,1,0:T(8,128)S(1)} %slice_bitcast_fusion.5), channel_id=1, source_target_pairs={{0,1},{1,0},{2,3},{3,2},{4,5},{5,4},{6,7},{7,6},{8,9},{9,8},{10,11... | collective-permute-start | bytes 49160 | tf_op jit(solution)/shard_map/ppermute | solution.py:405
  50.7 43.1 %collective-permute-start.8 = (bf16[64,4096]{1,0:T(8,128)(2,1)}, bf16[64,4096]{1,0:T(8,128)(2,1)S(1)}, u32[]{:S(2)}, u32[]{:S(2)}) collective-permute-start(bf16[64,4096]{1,0:T(8,128)(2,1)} %collective-permute-done.7.refs_4_), channel_id=1, source_target_pairs={{0,1},{1,0},{2,3},{3,2},{4,5},{5,4},{6,7},{7,6},{8,9},{9,8},{10,11... | collective-permute-start | bytes 1572872 | tf_op jit(solution)/shard_map/ppermute | solution.py:401
  51.5 1.0 copy-start.3
  63.1 2.5 %copy-start.4 = (bf16[64,4096]{1,0:T(8,128)(2,1)S(1)}, bf16[64,4096]{1,0:T(8,128)(2,1)}, u32[]{:S(2)}) copy-start(bf16[64,4096]{1,0:T(8,128)(2,1)} %shard_map.80.refs_2_) | copy-start | bytes 1572868
  63.1 30.8 %collective-permute-start.13 = (bf16[2,128,1024]{2,1,0:T(8,128)(2,1)S(1)}, bf16[2,128,1024]{2,1,0:T(8,128)(2,1)S(1)}, u32[]{:S(2)}, u32[]{:S(2)}) collective-permute-start(bf16[2,128,1024]{2,1,0:T(8,128)(2,1)S(1)} %shard_map.81.refs_4_), channel_id=1, source_target_pairs={{0,2},{2,0},{1,3},{3,1},{4,6},{6,4},{5,7},{7,5},{8,10},{10,8},{9,1... | collective-permute-start | bytes 1572872 | tf_op jit(solution)/shard_map/ppermute | solution.py:426
  64.7 54.1 %copy-start.10 = (bf16[64,4096]{1,0:T(8,128)(2,1)}, bf16[64,4096]{1,0:T(8,128)(2,1)S(1)}, u32[]{:S(2)}) copy-start(bf16[64,4096]{1,0:T(8,128)(2,1)S(1)} %collective-permute-done.9.refs_6_) | copy-start | bytes 1572868
  64.7 29.2 %collective-permute-start.10 = (bf16[64,4096]{1,0:T(8,128)(2,1)S(1)}, bf16[64,4096]{1,0:T(8,128)(2,1)S(1)}, u32[]{:S(2)}, u32[]{:S(2)}) collective-permute-start(bf16[64,4096]{1,0:T(8,128)(2,1)S(1)} %collective-permute-done.9.refs_6_), channel_id=1, source_target_pairs={{0,1},{1,0},{2,3},{3,2},{4,5},{5,4},{6,7},{7,6},{8,9},{9,8},{10,11... | collective-permute-start | bytes 1572872 | tf_op jit(solution)/shard_map/ppermute | solution.py:402
  79.9 38.8 %collective-permute-start.15 = (bf16[2,128,1536]{2,1,0:T(8,128)(2,1)S(1)}, bf16[2,128,1536]{2,1,0:T(8,128)(2,1)S(1)}, u32[]{:S(2)}, u32[]{:S(2)}) collective-permute-start(bf16[2,128,1536]{2,1,0:T(8,128)(2,1)S(1)} %shard_map.83.refs_4_), channel_id=1, source_target_pairs={{0,2},{2,0},{1,3},{3,1},{4,6},{6,4},{5,7},{7,5},{8,10},{10,8},{9,1... | collective-permute-start | bytes 2359304 | tf_op jit(solution)/shard_map/ppermute | solution.py:426
  81.3 30.5 %collective-permute-start.18 = (bf16[34,16,128]{2,1,0:T(8,128)(2,1)S(1)}, bf16[34,16,128]{2,1,0:T(8,128)(2,1)S(1)}, u32[]{:S(2)}, u32[]{:S(2)}) collective-permute-start(bf16[34,16,128]{2,1,0:T(8,128)(2,1)S(1)} %get-tuple-element.19), channel_id=1, source_target_pairs={{0,12},{4,8},{8,4},{12,0},{1,13},{5,9},{9,5},{13,1},{2,14},{6,10},... | collective-permute-start | bytes 417800 | tf_op jit(solution)/shard_map/ppermute | solution.py:409
  93.8 24.9 %copy-start.12 = (bf16[64,4096]{1,0:T(8,128)(2,1)}, bf16[64,4096]{1,0:T(8,128)(2,1)S(1)}, u32[]{:S(2)}) copy-start(bf16[64,4096]{1,0:T(8,128)(2,1)S(1)} %collective-permute-done.8.refs_5_) | copy-start | bytes 1572868
  93.8 24.9 %copy-start.14 = (bf16[64,4096]{1,0:T(8,128)(2,1)}, bf16[64,4096]{1,0:T(8,128)(2,1)S(1)}, u32[]{:S(2)}) copy-start(bf16[64,4096]{1,0:T(8,128)(2,1)S(1)} %collective-permute-done.10.refs_7_) | copy-start | bytes 1572868
  93.9 13.6 %copy-start.17 = (bf16[2,128,1024]{2,1,0:T(8,128)(2,1)}, bf16[2,128,1024]{2,1,0:T(8,128)(2,1)S(1)}, u32[]{:S(2)}) copy-start(bf16[2,128,1024]{2,1,0:T(8,128)(2,1)S(1)} %collective-permute-done.13.refs_9_.near_ref) | copy-start | bytes 1572868
  107.5 29.6 %copy-start.7 = (bf16[2,256,1024]{2,1,0:T(8,128)(2,1)}, bf16[2,256,1024]{2,1,0:T(8,128)(2,1)S(1)}, u32[]{:S(2)}) copy-start(bf16[2,256,1024]{2,1,0:T(8,128)(2,1)S(1)} %get-tuple-element.12.held_ref.kept_ref.refs_8_) | copy-start | bytes 3145732
  107.5 32.2 %collective-permute-start.14 = (bf16[2,128,1024]{2,1,0:T(8,128)(2,1)}, bf16[2,128,1024]{2,1,0:T(8,128)(2,1)S(1)}, u32[]{:S(2)}, u32[]{:S(2)}) collective-permute-start(bf16[2,128,1024]{2,1,0:T(8,128)(2,1)} %get-tuple-element.13), channel_id=1, source_target_pairs={{0,2},{2,0},{1,3},{3,1},{4,6},{6,4},{5,7},{7,5},{8,10},{10,8},{9,1... | collective-permute-start | bytes 1572872 | tf_op jit(solution)/shard_map/ppermute | solution.py:435
  109.1 34.0 %collective-permute-start.20 = (bf16[2,128,1024]{2,1,0:T(8,128)(2,1)}, bf16[2,128,1024]{2,1,0:T(8,128)(2,1)}, u32[]{:S(2)}, u32[]{:S(2)}) collective-permute-start(bf16[2,128,1024]{2,1,0:T(8,128)(2,1)} %shard_map.84.refs_8_), channel_id=1, source_target_pairs={{0,2},{2,0},{1,3},{3,1},{4,6},{6,4},{5,7},{7,5},{8,10},{10,8},{9,1... | collective-permute-start | bytes 1572872 | tf_op jit(solution)/shard_map/ppermute | solution.py:426
  109.6 8.9 %collective-permute-start.17 = (bf16[34,16,128]{2,1,0:T(8,128)(2,1)S(1)}, bf16[34,16,128]{2,1,0:T(8,128)(2,1)S(1)}, u32[]{:S(2)}, u32[]{:S(2)}) collective-permute-start(bf16[34,16,128]{2,1,0:T(8,128)(2,1)S(1)} %get-tuple-element.20), channel_id=1, source_target_pairs={{0,8},{4,12},{8,0},{12,4},{1,9},{5,13},{9,1},{13,5},{2,10},{6,14},... | collective-permute-start | bytes 417800 | tf_op jit(solution)/shard_map/ppermute | solution.py:409
  111.8 31.3 %copy-start.18 = (bf16[34,16,128]{2,1,0:T(8,128)(2,1)}, bf16[34,16,128]{2,1,0:T(8,128)(2,1)S(1)}, u32[]{:S(2)}) copy-start(bf16[34,16,128]{2,1,0:T(8,128)(2,1)S(1)} %collective-permute-done.18.refs_12_.refs_3_) | copy-start | bytes 417796
  111.8 7.0 %collective-permute-start.16 = (bf16[34,16,128]{2,1,0:T(8,128)(2,1)S(1)}, bf16[34,16,128]{2,1,0:T(8,128)(2,1)S(1)}, u32[]{:S(2)}, u32[]{:S(2)}) collective-permute-start(bf16[34,16,128]{2,1,0:T(8,128)(2,1)S(1)} %get-tuple-element.21), channel_id=1, source_target_pairs={{0,4},{4,0},{8,12},{12,8},{1,5},{5,1},{9,13},{13,9},{2,6},{6,2},{1... | collective-permute-start | bytes 417800 | tf_op jit(solution)/shard_map/ppermute | solution.py:409
  118.5 24.5 %copy-start.19 = (bf16[34,16,128]{2,1,0:T(8,128)(2,1)}, bf16[34,16,128]{2,1,0:T(8,128)(2,1)S(1)}, u32[]{:S(2)}) copy-start(bf16[34,16,128]{2,1,0:T(8,128)(2,1)S(1)} %collective-permute-done.17.refs_11_.refs_2_) | copy-start | bytes 417796
  118.8 18.3 %copy-start.20 = (bf16[34,16,128]{2,1,0:T(8,128)(2,1)}, bf16[34,16,128]{2,1,0:T(8,128)(2,1)S(1)}, u32[]{:S(2)}) copy-start(bf16[34,16,128]{2,1,0:T(8,128)(2,1)S(1)} %collective-permute-done.16.refs_10_.refs_1_) | copy-start | bytes 417796
  118.8 18.3 %copy-start.16 = (bf16[2,128,1536]{2,1,0:T(8,128)(2,1)}, bf16[2,128,1536]{2,1,0:T(8,128)(2,1)S(1)}, u32[]{:S(2)}) copy-start(bf16[2,128,1536]{2,1,0:T(8,128)(2,1)S(1)} %collective-permute-done.15.refs_9_.near_ref) | copy-start | bytes 2359300
  137.1 1.2 copy-start.8
  138.3 34.1 %collective-permute-start.19 = (bf16[2,128,1536]{2,1,0:T(8,128)(2,1)}, bf16[2,128,1536]{2,1,0:T(8,128)(2,1)}, u32[]{:S(2)}, u32[]{:S(2)}) collective-permute-start(bf16[2,128,1536]{2,1,0:T(8,128)(2,1)} %get-tuple-element.15), channel_id=1, source_target_pairs={{0,2},{2,0},{1,3},{3,1},{4,6},{6,4},{5,7},{7,5},{8,10},{10,8},{9,1... | collective-permute-start | bytes 2359304 | tf_op jit(solution)/shard_map/ppermute | solution.py:435
  139.8 0.8 copy-start.24
  140.6 2.5 %copy-start.11 = (bf16[64,4096]{1,0:T(8,128)(2,1)S(1)}, bf16[64,4096]{1,0:T(8,128)(2,1)}, u32[]{:S(2)}) copy-start(bf16[64,4096]{1,0:T(8,128)(2,1)} %copy-done.10) | copy-start | bytes 1572868
  140.6 2.5 %copy-start.13 = (bf16[64,4096]{1,0:T(8,128)(2,1)S(1)}, bf16[64,4096]{1,0:T(8,128)(2,1)}, u32[]{:S(2)}) copy-start(bf16[64,4096]{1,0:T(8,128)(2,1)} %copy-done.12) | copy-start | bytes 1572868
  143.1 1.5 copy-start.1
  144.6 1.4 copy-start.9
  146.0 1.0 copy-start.15
  147.0 0.9 copy-start.21
  161.6 1.0 copy-start.22
  162.6 13.6 %collective-permute-start.21 = (bf16[2,128,1024]{2,1,0:T(8,128)(2,1)}, bf16[2,128,1024]{2,1,0:T(8,128)(2,1)S(1)}, u32[]{:S(2)}, u32[]{:S(2)}) collective-permute-start(bf16[2,128,1024]{2,1,0:T(8,128)(2,1)} %get-tuple-element.17), channel_id=1, source_target_pairs={{0,2},{2,0},{1,3},{3,1},{4,6},{6,4},{5,7},{7,5},{8,10},{10,8},{9,1... | collective-permute-start | bytes 1572872 | tf_op jit(solution)/shard_map/ppermute | solution.py:435
  176.1 0.8 copy-start.23

commit v3 on v2

--- a/solution.py
+++ b/solution.py
@@ -14,6 +14,7 @@
 f32 = jnp.float32
 bf16 = jnp.bfloat16
 VMEM = 44 << 20
+TOKEN = jax.ShapeDtypeStruct((8, 128), jnp.float32)
 SHORT = pl.CostEstimate(flops=1, bytes_accessed=1, transcendentals=0)
 
 
@@ -33,7 +34,13 @@
     )(x, *tokens)
 
 
-def attention_kernel(limits_ref, place_ref, mine_ref, other_ref, kv_ref, num_ref, stat_ref):
+def token_spec():
+    return pl.BlockSpec(TOKEN.shape, lambda *_: (0, 0))
+
+
+def attention_kernel(
+    limits_ref, place_ref, mine_ref, other_ref, kv_ref, num_ref, stat_ref, token_ref
+):
     chips, per_step, rows, _ = mine_ref.shape
     slots = kv_ref.shape[1]
     half = kv_ref.shape[2] // 2
@@ -42,6 +49,7 @@
     gx, gz = place_ref[0], place_ref[1]
     slot = lax.broadcasted_iota(jnp.int32, (slots, total), 0)
     zero = jnp.zeros((2 * rows, HD), bf16)
+    token_ref[...] = jnp.zeros_like(token_ref)
     tops, sums = [], []
     for i in range(per_step):
         limit = limits_ref[step * per_step + i]
@@ -94,11 +102,13 @@
             out_specs=[
                 pl.BlockSpec((2, chips, per_step, rows, HD), lambda j, *_: (0, 0, j, 0, 0)),
                 pl.BlockSpec((2, chips, 2, per_step, rows), lambda j, *_: (0, 0, 0, j, 0)),
+                token_spec(),
             ],
         ),
         out_shape=[
             jax.ShapeDtypeStruct((2, chips, sequences, rows, HD), bf16),
             jax.ShapeDtypeStruct((2, chips, 2, sequences, rows), f32),
+            TOKEN,
         ],
         compiler_params=pltpu.CompilerParams(vmem_limit_bytes=VMEM),
         cost_estimate=SHORT,
@@ -113,8 +123,9 @@
     return parts
 
 
-def pair_kernel(num_ref, other_num_ref, stat_ref, other_stat_ref, out_ref):
+def pair_kernel(num_ref, other_num_ref, stat_ref, other_stat_ref, out_ref, token_ref):
     chips, sequences = num_ref.shape[1:3]
+    token_ref[...] = jnp.zeros_like(token_ref)
     for c in range(chips):
         top = jnp.maximum(stat_ref[0, c, 0], other_stat_ref[c, 0])
         left = jnp.exp(stat_ref[0, c, 0] - top)
@@ -145,8 +156,8 @@
         pair_kernel,
         grid=(1,),
         in_specs=[first, rest, first_stat, rest_stat],
-        out_specs=pl.BlockSpec(out_shape, lambda j: (0, 0, 0, 0)),
-        out_shape=jax.ShapeDtypeStruct(out_shape, bf16),
+        out_specs=[pl.BlockSpec(out_shape, lambda j: (0, 0, 0, 0)), token_spec()],
+        out_shape=[jax.ShapeDtypeStruct(out_shape, bf16), TOKEN],
         compiler_params=pltpu.CompilerParams(vmem_limit_bytes=VMEM),
         cost_estimate=SHORT,
     )(num, other_num, stat, other_stat)
@@ -227,9 +238,9 @@
 
 
 def product_kernel(place_ref, *refs, count, cuts, pieces):
-    x_ref, sems, x_sems, flat = refs[-4:]
-    outs = refs[-4 - len(cuts) : -4]
-    left_ref, right_ref = refs[-6 - len(cuts) : -4 - len(cuts)]
+    token_ref, x_ref, sems, x_sems, flat = refs[-5:]
+    outs = refs[-5 - len(cuts) : -5]
+    left_ref, right_ref = refs[-7 - len(cuts) : -5 - len(cuts)]
     block = x_ref.shape[0] // (2 * len(pieces))
     gz, to_send = place_ref[1], place_ref[2]
     j = pl.program_id(0)
@@ -281,6 +292,7 @@
                 x, jnp.concatenate([s[0] for s in sides], 1), preferred_element_type=f32
             )
             up += jnp.dot(x, jnp.concatenate([s[1] for s in sides], 1), preferred_element_type=f32)
+        token_ref[...] = jnp.zeros_like(token_ref)
         low = 0
         for ref, high in zip(outs, cuts):
             ref[0] = gate[low:high].astype(bf16)
@@ -320,7 +332,8 @@
             out_specs=[
                 pl.BlockSpec((2, size, 256), lambda j, _: (0, 0, jnp.maximum(j - 1, 0)))
                 for size in sizes
-            ],
+            ]
+            + [token_spec()],
             scratch_shapes=[
                 pltpu.VMEM((rows, depth), bf16),
                 pltpu.SemaphoreType.DMA((2, 2)),
@@ -328,13 +341,14 @@
                 pltpu.VMEM((2, 2, 2 * depth, 128), bf16),
             ],
         ),
-        out_shape=[jax.ShapeDtypeStruct((2, size, count * 256), bf16) for size in sizes],
+        out_shape=[jax.ShapeDtypeStruct((2, size, count * 256), bf16) for size in sizes] + [TOKEN],
         compiler_params=pltpu.CompilerParams(vmem_limit_bytes=VMEM),
         cost_estimate=SHORT,
     )(place, *blocks, *tokens, weights, weights)
 
 
-def gated_kernel(swap_ref, held_ref, kept_ref, near_ref, far_ref, out_ref):
+def gated_kernel(swap_ref, held_ref, kept_ref, near_ref, far_ref, out_ref, token_ref):
+    token_ref[...] = jnp.zeros_like(token_ref)
     half = near_ref.shape[1]
     for i, theirs in enumerate((near_ref, far_ref)):
         rows = slice(i * half, (i + 1) * half)
@@ -358,9 +372,12 @@
                 pl.BlockSpec((2, half, wide), lambda j, _: (0, 0, j)),
                 pl.BlockSpec((2, half, wide), lambda j, _: (0, 0, j)),
             ],
-            out_specs=pl.BlockSpec((rows, wide), lambda j, _: (0, first * 256 // wide + j)),
+            out_specs=[
+                pl.BlockSpec((rows, wide), lambda j, _: (0, first * 256 // wide + j)),
+                token_spec(),
+            ],
         ),
-        out_shape=jax.ShapeDtypeStruct((rows, width), bf16),
+        out_shape=[jax.ShapeDtypeStruct((rows, width), bf16), TOKEN],
         input_output_aliases={} if held is None else {1: 0},
         cost_estimate=SHORT,
     )(swap, kept if held is None else held, kept, near, far)
@@ -393,7 +410,7 @@
     )
     other_q = lax.ppermute(all_q, "gz", over)
     limits = jnp.clip(lengths - me * slots, 0, slots)
-    num, stat = cached_attention(all_q, other_q, kv_cache, limits, place)
+    num, stat, _ = cached_attention(all_q, other_q, kv_cache, limits, place)
 
     along = after(along, num)
     along_other = lax.ppermute(along, "gz", over)
@@ -403,7 +420,7 @@
 
     other_num = lax.ppermute(num[1], "gz", over)
     other_stat = lax.ppermute(stat[1], "gz", over)
-    pair = join_pair(num, other_num, stat, other_stat)
+    pair, _ = join_pair(num, other_num, stat, other_stat)
     nums = [pair[0]]
     for bit in range(1, chips):
         nums.append(lax.ppermute(pair[bit], "gx", xor_pairs("gx", bit)))
@@ -421,8 +438,8 @@
     near, tokens = [], (num,)
     blocks = (mine, mine_other, along, along_other)
     pieces = (((0, 1), (2, 3)),)
-    for i, (first, last) in enumerate(spans):
-        (out,) = product(place, blocks, pieces, weights, first, last, (half,), *tokens)
+    for first, last in spans:
+        out, done = product(place, blocks, pieces, weights, first, last, (half,), *tokens)
         near.append(lax.ppermute(out, "gy", over))
         tokens = (out, pair)
     blocks += (mine_far, mine_far_other, along_far, along_far_other)
@@ -431,15 +448,17 @@
     hidden_units = None
     waiting = []
     for i, (first, last) in enumerate(spans):
-        sent, keep = product(place, blocks, pieces, weights, first, last, (half, 3 * half), *tokens)
+        sent, keep, done = product(
+            place, blocks, pieces, weights, first, last, (half, 3 * half), *tokens
+        )
         waiting.append((keep, near[i], lax.ppermute(sent, "gy", over), first))
-        tokens = (keep, near[min(i + 1, len(near) - 1)], *nums[1:])
+        tokens = (done, near[1], *nums[1:]) if i == 0 else (done, near[-1])
         if i + 1 >= len(spans) - 1 and len(waiting) > 1:
             keep, early, late, start = waiting.pop(0)
-            hidden_units = gated(keep, early, late, swap, hidden_units, start, width)
-            tokens += (hidden_units,)
+            hidden_units, done = gated(keep, early, late, swap, hidden_units, start, width)
+            tokens += (done,)
     for keep, early, late, start in waiting:
-        hidden_units = gated(keep, early, late, swap, hidden_units, start, width)
+        hidden_units, _ = gated(keep, early, late, swap, hidden_units, start, width)
 
     attended = attended.reshape(sequences, steps, heads, HD).transpose(1, 0, 2, 3)
     return hidden_units, attended.reshape(steps, sequences, heads * HD)

time: 180 us -> 177 us (0.983)
  local copies, waits for them, and re-layouts: 17.7 us -> 12.9 us
  Pallas kernels: 117 us -> 119 us
    unnamed x54 -> x50, local copies, waits for them, and re-layouts: 13.9 us -> 9.09 us
  transfers between devices with their start and end apart: 22 -> 22, of which waited for: 6 -> 7; matrix products, arithmetic and copies ran while one was open for 2% -> 2% of each run, Pallas kernels for 62% -> 65%
where the time goes in v3:
time: 177 us; the launch traced here: 176 us
  Pallas kernels  119 us (67%)
  waiting for transfers between devices  22.6 us (13%)
  starting transfers between devices  20.2 us (11%)
  local copies, waits for them, and re-layouts  12.9 us (7%)
    pallas_call x6, Pallas kernels, product(): pl.pallas_call(functools.partial(product_kernel, count=count, cuts=cuts,...  82.7 us
    pallas_call x1, Pallas kernels, cached_attention(): pl.pallas_call(attention_kernel, grid_spec=pltpu.PrefetchScalarGridSpec(n...  17.7 us
    ppermute x3, waiting for transfers between devices, on_device(): lax.ppermute(my_q, 'gx', xor_pairs('gx', bit))  10.7 us
    unnamed x50, local copies, waits for them, and re-layouts  9.09 us
    pallas_call x3, Pallas kernels, gated(): pl.pallas_call(gated_kernel, grid_spec=pltpu.PrefetchScalarGridSpec(num_s...  8.49 us
    ppermute x3, waiting for transfers between devices, on_device(): nums.append(lax.ppermute(pair[bit], 'gx', xor_pairs('gx', bit)))  6.12 us
    pallas_call x1, Pallas kernels, join_all(): pl.pallas_call(functools.partial(final_kernel, count=len(nums)), out_shap...  6.04 us
    ppermute x3, starting transfers between devices, on_device(): lax.ppermute(my_q, 'gx', xor_pairs('gx', bit))  5.62 us
  transfers between devices with their start and end apart: 22, of which 7 were waited for; matrix products, arithmetic and copies ran while one was open for 2% of the time, Pallas kernels for 65%

profile of v3, /device:TPU:0, one launch (start us, length us, event | category | flops | bytes accessed | tf_op | source)
XLA Modules:
  0.0 176.3 jit_solution(18391572236286726241)
XLA Ops:
  0.6 0.9 copy.19
  1.6 0.7 copy_bitcast_fusion.refs_0_
  2.3 2.3 %shard_map.77.refs_1_.refs_0_ = bf16[64,4096]{1,0:T(8,128)(2,1)} custom-call(bf16[64,4096]{1,0:T(8,128)(2,1)} %x_ref.1), custom_call_target="tpu_custom_call" | custom-call | flops 1 | bytes 1 | tf_op jit(solution)/shard_map/pallas_call | solution.py:223
  4.6 5.0 %collective-permute-start.4 = (bf16[1,32,16,128]{3,2,1,0:T(8,128)(2,1)}, bf16[1,32,16,128]{3,2,1,0:T(8,128)(2,1)S(1)}, u32[]{:S(2)}, u32[]{:S(2)}) collective-permute-start(bf16[1,32,16,128]{3,2,1,0:T(8,128)(2,1)} %shard_map.78), channel_id=1, source_target_pairs={{0,12},{4,8},{8,4},{12,0},{1,13},{5,9},{9,5},{13,1},{2,14},{6,10},... | collective-permute-start | bytes 393224 | tf_op jit(solution)/shard_map/ppermute | solution.py:409
  9.6 0.6 collective-permute-start.2
  10.2 4.1 %collective-permute-done.4 = bf16[1,32,16,128]{3,2,1,0:T(8,128)(2,1)S(1)} collective-permute-done((bf16[1,32,16,128]{3,2,1,0:T(8,128)(2,1)}, bf16[1,32,16,128]{3,2,1,0:T(8,128)(2,1)S(1)}, u32[]{:S(2)}, u32[]{:S(2)}) %collective-permute-start.4) | collective-permute-done | bytes 131104 | tf_op jit(solution)/shard_map/ppermute | solution.py:409
  14.3 6.6 %collective-permute-done.3 = bf16[1,32,16,128]{3,2,1,0:T(8,128)(2,1)S(1)} collective-permute-done((bf16[1,32,16,128]{3,2,1,0:T(8,128)(2,1)}, bf16[1,32,16,128]{3,2,1,0:T(8,128)(2,1)S(1)}, u32[]{:S(2)}, u32[]{:S(2)}) %collective-permute-start.3) | collective-permute-done | bytes 131104 | tf_op jit(solution)/shard_map/ppermute | solution.py:409
  20.9 1.0 pad_maximum_fusion.mine_ref
  22.1 3.0 %collective-permute-start.7 = (bf16[64,4096]{1,0:T(8,128)(2,1)}, bf16[64,4096]{1,0:T(8,128)(2,1)}, u32[]{:S(2)}, u32[]{:S(2)}) collective-permute-start(bf16[64,4096]{1,0:T(8,128)(2,1)} %shard_map.77.refs_1_.refs_0_), channel_id=1, source_target_pairs={{0,4},{4,0},{8,12},{12,8},{1,5},{5,1},{9,13},{13,9},{2,6},{6,2},{1... | collective-permute-start | bytes 1572872 | tf_op jit(solution)/shard_map/ppermute | solution.py:398
  25.2 17.7 %shard_map.79 = (bf16[2,4,32,16,128]{4,3,2,1,0:T(8,128)(2,1)S(1)}, f32[2,4,2,32,16]{4,3,2,1,0:T(8,128)S(1)}, f32[8,128]{1,0:T(8,128)}) custom-call(s32[32]{0:T(128)S(1)} %subtract_clamp_fusion.limits_ref, s32[3]{0:T(128)S(1)} %pad_add_fusion.place_ref, bf16[4,32,16,128]{3,2,1,0:T(8,128)(2,1)S(1)} %pad_maximum_fusion.mine_ref, ...), custom_call_target="tpu_custom_call" | custom-call | flops 1 | bytes 1 | tf_op jit(solution)/shard_map/pallas_call | solution.py:92
  42.9 1.0 copy-done.4
  43.8 4.8 %collective-permute-done.1.refs_0_ = bf16[64,4096]{1,0:T(8,128)(2,1)S(1)} collective-permute-done((bf16[64,4096]{1,0:T(8,128)(2,1)}, bf16[64,4096]{1,0:T(8,128)(2,1)S(1)}, u32[]{:S(2)}, u32[]{:S(2)}) %collective-permute-start.1) | collective-permute-done | bytes 524320 | tf_op jit(solution)/shard_map/ppermute | solution.py:397
  48.6 0.8 copy-done.1
  49.4 0.6 copy-done.5
  50.2 0.6 collective-permute-start.12
  50.8 0.7 collective-permute-done.6.refs_3_
  51.5 1.0 copy-done.2
  52.6 11.1 %shard_map.81 = (bf16[2,128,1024]{2,1,0:T(8,128)(2,1)S(1)}, f32[8,128]{1,0:T(8,128)}) custom-call(s32[3]{0:T(128)S(1)} %pad_add_fusion.place_ref, bf16[64,4096]{1,0:T(8,128)(2,1)S(1)} %copy-done, bf16[64,4096]{1,0:T(8,128)(2,1)S(1)} %collective-permute-done.refs_1_, bf16[64,4096]{1,0:T(8,128)(2,1)S(1)} %copy-done.2, ...), custom_call_target="tpu_custom_call" | custom-call | flops 1 | bytes 1 | tf_op jit(solution)/shard_map/pallas_call | solution.py:326
  63.7 1.6 collective-permute-start.13
  65.3 1.4 shard_map.82
  66.7 14.9 %shard_map.83 = (bf16[2,128,1536]{2,1,0:T(8,128)(2,1)S(1)}, f32[8,128]{1,0:T(8,128)}) custom-call(s32[3]{0:T(128)S(1)} %pad_add_fusion.place_ref, bf16[64,4096]{1,0:T(8,128)(2,1)S(1)} %copy-done, bf16[64,4096]{1,0:T(8,128)(2,1)S(1)} %collective-permute-done.refs_1_, bf16[64,4096]{1,0:T(8,128)(2,1)S(1)} %copy-done.3, ...), custom_call_target="tpu_custom_call" | custom-call | flops 1 | bytes 1 | tf_op jit(solution)/shard_map/pallas_call | solution.py:326
  81.6 0.6 collective-permute-start.15
  82.2 0.7 slice_bitcast_fusion.1
  82.9 1.3 collective-permute-start.18
  84.3 11.2 %shard_map.84 = (bf16[2,128,1024]{2,1,0:T(8,128)(2,1)}, f32[8,128]{1,0:T(8,128)}) custom-call(s32[3]{0:T(128)S(1)} %pad_add_fusion.place_ref, bf16[64,4096]{1,0:T(8,128)(2,1)S(1)} %copy-done, bf16[64,4096]{1,0:T(8,128)(2,1)S(1)} %collective-permute-done.refs_1_, bf16[64,4096]{1,0:T(8,128)(2,1)S(1)} %copy-done.3, ...), custom_call_target="tpu_custom_call" | custom-call | flops 1 | bytes 1 | tf_op jit(solution)/shard_map/pallas_call | solution.py:326
  95.5 13.6 %shard_map.85 = (bf16[2,128,1024]{2,1,0:T(8,128)(2,1)}, bf16[2,256,1024]{2,1,0:T(8,128)(2,1)S(1)}, f32[8,128]{1,0:T(8,128)S(1)}) custom-call(s32[3]{0:T(128)S(1)} %pad_add_fusion.place_ref, bf16[64,4096]{1,0:T(8,128)(2,1)S(1)} %copy-done, bf16[64,4096]{1,0:T(8,128)(2,1)S(1)} %collective-permute-done.refs_1_, bf16[64,4096]{1,0:T(8,128)(2,1)S(1)} %copy-done.3, ...), custom_call_target="tpu_custom_call" | custom-call | flops 1 | bytes 1 | tf_op jit(solution)/shard_map/pallas_call | solution.py:326
  109.2 1.5 collective-permute-start.14
  110.7 0.5 collective-permute-start.20
  111.3 2.2 %collective-permute-start.17 = (bf16[34,16,128]{2,1,0:T(8,128)(2,1)S(1)}, bf16[34,16,128]{2,1,0:T(8,128)(2,1)S(1)}, u32[]{:S(2)}, u32[]{:S(2)}) collective-permute-start(bf16[34,16,128]{2,1,0:T(8,128)(2,1)S(1)} %get-tuple-element.40), channel_id=1, source_target_pairs={{0,8},{4,12},{8,0},{12,4},{1,9},{5,13},{9,1},{13,5},{2,10},{6,14},... | collective-permute-start | bytes 417800 | tf_op jit(solution)/shard_map/ppermute | solution.py:426
  113.4 0.9 collective-permute-start.16
  114.3 5.9 %collective-permute-done.17.refs_11_.refs_2_ = bf16[34,16,128]{2,1,0:T(8,128)(2,1)S(1)} collective-permute-done((bf16[34,16,128]{2,1,0:T(8,128)(2,1)S(1)}, bf16[34,16,128]{2,1,0:T(8,128)(2,1)S(1)}, u32[]{:S(2)}, u32[]{:S(2)}) %collective-permute-start.17) | collective-permute-done | bytes 139296 | tf_op jit(solution)/shard_map/ppermute | solution.py:426
  120.2 0.2 collective-permute-done.16.refs_10_.refs_1_
  120.5 18.3 %shard_map.87 = (bf16[2,128,1536]{2,1,0:T(8,128)(2,1)}, bf16[2,256,1536]{2,1,0:T(8,128)(2,1)S(1)}, f32[8,128]{1,0:T(8,128)S(1)}) custom-call(s32[3]{0:T(128)S(1)} %pad_add_fusion.place_ref, bf16[64,4096]{1,0:T(8,128)(2,1)S(1)} %copy-done, bf16[64,4096]{1,0:T(8,128)(2,1)S(1)} %collective-permute-done.refs_1_, bf16[64,4096]{1,0:T(8,128)(2,1)S(1)} %copy-done.3, ...), custom_call_target="tpu_custom_call" | custom-call | flops 1 | bytes 1 | tf_op jit(solution)/shard_map/pallas_call | solution.py:326
  138.8 1.2 copy-done.15
  140.0 1.5 collective-permute-start.19
  141.4 2.4 %shard_map.86 = (bf16[256,3584]{1,0:T(8,128)(2,1)}, f32[8,128]{1,0:T(8,128)}) custom-call(s32[1]{0:T(128)} %bitcast.swap_ref, bf16[2,256,1024]{2,1,0:T(8,128)(2,1)} %copy-done.12, bf16[2,256,1024]{2,1,0:T(8,128)(2,1)} %copy-done.12, bf16[2,128,1024]{2,1,0:T(8,128)(2,1)} %copy-done.14, bf16[2,128,1024]{2,1,0:T(8,128)(2,1)} %collective-permute-done.14.far_ref), custom_call_target="tpu_custom_call" | custom-call | flops 1 | bytes 1 | tf_op jit(solution)/shard_map/pallas_call | solution.py:364
  143.9 1.0 copy-done.11
  144.9 0.7 copy-done.20
  145.6 13.6 %shard_map.89 = (bf16[2,128,1024]{2,1,0:T(8,128)(2,1)}, bf16[2,256,1024]{2,1,0:T(8,128)(2,1)S(1)}, f32[8,128]{1,0:T(8,128)}) custom-call(s32[3]{0:T(128)S(1)} %pad_add_fusion.place_ref, bf16[64,4096]{1,0:T(8,128)(2,1)S(1)} %copy-done, bf16[64,4096]{1,0:T(8,128)(2,1)S(1)} %collective-permute-done.refs_1_, bf16[64,4096]{1,0:T(8,128)(2,1)S(1)} %copy-done.3, ...), custom_call_target="tpu_custom_call" | custom-call | flops 1 | bytes 1 | tf_op jit(solution)/shard_map/pallas_call | solution.py:326
  159.2 1.0 copy-done.16
  160.2 0.6 collective-permute-start.21
  160.9 0.6 copy_bitcast_fusion.1
  161.5 6.0 %shard_map.91 = bf16[32,16,128]{2,1,0:T(8,128)(2,1)} custom-call(bf16[34,16,128]{2,1,0:T(8,128)(2,1)} %get-tuple-element.38.refs_0_, bf16[34,16,128]{2,1,0:T(8,128)(2,1)} %copy-done.19, bf16[34,16,128]{2,1,0:T(8,128)(2,1)} %copy-done.18, bf16[34,16,128]{2,1,0:T(8,128)(2,1)} %copy-done.17, bf16[32,16,128]{2,1,0:T(8,128)(2,1)} %bitcast.59, ...), custom_call_target="tpu_custom_call" | custom-call | flops 1 | bytes 1 | tf_op jit(solution)/shard_map/pallas_call | solution.py:201
  167.5 0.9 reshape.33
  168.5 0.7 copy.16
  169.2 3.7 %shard_map.88 = (bf16[256,3584]{1,0:T(8,128)(2,1)}, f32[8,128]{1,0:T(8,128)}) custom-call(s32[1]{0:T(128)} %bitcast.swap_ref, bf16[256,3584]{1,0:T(8,128)(2,1)} %get-tuple-element.28.held_ref, bf16[2,256,1536]{2,1,0:T(8,128)(2,1)} %copy-done.15, bf16[2,128,1536]{2,1,0:T(8,128)(2,1)} %copy-done.13, ...), custom_call_target="tpu_custom_call", output_to_operand_aliasing={{0}: (1, {})} | custom-call | flops 1 | bytes 1 | tf_op jit(solution)/shard_map/pallas_call | solution.py:364
  173.1 0.8 copy-done.21
  173.9 2.4 %shard_map.90 = (bf16[256,3584]{1,0:T(8,128)(2,1)}, f32[8,128]{1,0:T(8,128)}) custom-call(s32[1]{0:T(128)} %bitcast.swap_ref, bf16[256,3584]{1,0:T(8,128)(2,1)} %get-tuple-element.32.held_ref, bf16[2,256,1024]{2,1,0:T(8,128)(2,1)} %copy-done.16, bf16[2,128,1024]{2,1,0:T(8,128)(2,1)} %collective-permute-done.20.refs_9_.near_ref, ...), custom_call_target="tpu_custom_call", output_to_operand_aliasing={{0}: (1, {})} | custom-call | flops 1 | bytes 1 | tf_op jit(solution)/shard_map/pallas_call | solution.py:364
  (72 shorter events, 0.9 us)
Async XLA Ops:
  0.6 24.5 %copy-start.23 = (s32[32]{0:T(128)S(1)}, s32[32]{0:T(128)}, u32[]{:S(2)}) copy-start(s32[32]{0:T(128)} %param.11) | copy-start | bytes 388
  4.6 9.7 %collective-permute-start.4 = (bf16[1,32,16,128]{3,2,1,0:T(8,128)(2,1)}, bf16[1,32,16,128]{3,2,1,0:T(8,128)(2,1)S(1)}, u32[]{:S(2)}, u32[]{:S(2)}) collective-permute-start(bf16[1,32,16,128]{3,2,1,0:T(8,128)(2,1)} %shard_map.78), channel_id=1, source_target_pairs={{0,12},{4,8},{8,4},{12,0},{1,13},{5,9},{9,5},{13,1},{2,14},{6,10},... | collective-permute-start | bytes 393224 | tf_op jit(solution)/shard_map/ppermute | solution.py:409
  9.6 11.3 %collective-permute-start.3 = (bf16[1,32,16,128]{3,2,1,0:T(8,128)(2,1)}, bf16[1,32,16,128]{3,2,1,0:T(8,128)(2,1)S(1)}, u32[]{:S(2)}, u32[]{:S(2)}) collective-permute-start(bf16[1,32,16,128]{3,2,1,0:T(8,128)(2,1)} %shard_map.78), channel_id=1, source_target_pairs={{0,8},{4,12},{8,0},{12,4},{1,9},{5,13},{9,1},{13,5},{2,10},{6,14},... | collective-permute-start | bytes 393224 | tf_op jit(solution)/shard_map/ppermute | solution.py:409
  9.6 11.3 %collective-permute-start.2 = (bf16[1,32,16,128]{3,2,1,0:T(8,128)(2,1)}, bf16[1,32,16,128]{3,2,1,0:T(8,128)(2,1)S(1)}, u32[]{:S(2)}, u32[]{:S(2)}) collective-permute-start(bf16[1,32,16,128]{3,2,1,0:T(8,128)(2,1)} %shard_map.78), channel_id=1, source_target_pairs={{0,4},{4,0},{8,12},{12,8},{1,5},{5,1},{9,13},{13,9},{2,6},{6,2},{1... | collective-permute-start | bytes 393224 | tf_op jit(solution)/shard_map/ppermute | solution.py:409
  21.9 3.3 %collective-permute-start.5 = (bf16[4,32,16,128]{3,2,1,0:T(8,128)(2,1)S(1)}, bf16[4,32,16,128]{3,2,1,0:T(8,128)(2,1)S(1)}, u32[]{:S(2)}, u32[]{:S(2)}) collective-permute-start(bf16[4,32,16,128]{3,2,1,0:T(8,128)(2,1)S(1)} %pad_maximum_fusion.mine_ref), channel_id=1, source_target_pairs={{0,1},{1,0},{2,3},{3,2},{4,5},{5,4},{6,7},{7,6},{8,9},{9,8},{10,11... | collective-permute-start | bytes 1572872 | tf_op jit(solution)/shard_map/ppermute | solution.py:411
  22.0 26.6 %collective-permute-start.1 = (bf16[64,4096]{1,0:T(8,128)(2,1)}, bf16[64,4096]{1,0:T(8,128)(2,1)S(1)}, u32[]{:S(2)}, u32[]{:S(2)}) collective-permute-start(bf16[64,4096]{1,0:T(8,128)(2,1)} %shard_map.77.refs_1_.refs_0_), channel_id=1, source_target_pairs={{0,8},{4,12},{8,0},{12,4},{1,9},{5,13},{9,1},{13,5},{2,10},{6,14},... | collective-permute-start | bytes 1572872 | tf_op jit(solution)/shard_map/ppermute | solution.py:397
  22.1 28.1 %collective-permute-start.7 = (bf16[64,4096]{1,0:T(8,128)(2,1)}, bf16[64,4096]{1,0:T(8,128)(2,1)}, u32[]{:S(2)}, u32[]{:S(2)}) collective-permute-start(bf16[64,4096]{1,0:T(8,128)(2,1)} %shard_map.77.refs_1_.refs_0_), channel_id=1, source_target_pairs={{0,4},{4,0},{8,12},{12,8},{1,5},{5,1},{9,13},{13,9},{2,6},{6,2},{1... | collective-permute-start | bytes 1572872 | tf_op jit(solution)/shard_map/ppermute | solution.py:398
  25.1 25.6 %collective-permute-start = (bf16[64,4096]{1,0:T(8,128)(2,1)}, bf16[64,4096]{1,0:T(8,128)(2,1)S(1)}, u32[]{:S(2)}, u32[]{:S(2)}) collective-permute-start(bf16[64,4096]{1,0:T(8,128)(2,1)} %shard_map.77.refs_1_.refs_0_), channel_id=1, source_target_pairs={{0,1},{1,0},{2,3},{3,2},{4,5},{5,4},{6,7},{7,6},{8,9},{9,8},{10,11... | collective-permute-start | bytes 1572872 | tf_op jit(solution)/shard_map/ppermute | solution.py:399
  42.9 1.0 copy-start.4
  43.8 7.7 %copy-start = (bf16[64,4096]{1,0:T(8,128)(2,1)S(1)}, bf16[64,4096]{1,0:T(8,128)(2,1)}, u32[]{:S(2)}) copy-start(bf16[64,4096]{1,0:T(8,128)(2,1)} %shard_map.77.refs_1_.refs_0_) | copy-start | bytes 1572868
  48.6 0.8 copy-start.1
  48.6 1.4 copy-start.5
  49.4 15.8 %collective-permute-start.9 = (bf16[64,4096]{1,0:T(8,128)(2,1)}, bf16[64,4096]{1,0:T(8,128)(2,1)S(1)}, u32[]{:S(2)}, u32[]{:S(2)}) collective-permute-start(bf16[64,4096]{1,0:T(8,128)(2,1)} %shard_map.80.refs_2_), channel_id=1, source_target_pairs={{0,4},{4,0},{8,12},{12,8},{1,5},{5,1},{9,13},{13,9},{2,6},{6,2},{1... | collective-permute-start | bytes 1572872 | tf_op jit(solution)/shard_map/ppermute | solution.py:417
  49.4 2.1 %collective-permute-start.6 = (bf16[64,4096]{1,0:T(8,128)(2,1)}, bf16[64,4096]{1,0:T(8,128)(2,1)S(1)}, u32[]{:S(2)}, u32[]{:S(2)}) collective-permute-start(bf16[64,4096]{1,0:T(8,128)(2,1)} %shard_map.80.refs_2_), channel_id=1, source_target_pairs={{0,1},{1,0},{2,3},{3,2},{4,5},{5,4},{6,7},{7,6},{8,9},{9,8},{10,11... | collective-permute-start | bytes 1572872 | tf_op jit(solution)/shard_map/ppermute | solution.py:416
  50.1 15.2 %collective-permute-start.11 = (bf16[4,32,16,128]{3,2,1,0:T(8,128)(2,1)S(1)}, bf16[4,32,16,128]{3,2,1,0:T(8,128)(2,1)S(1)}, u32[]{:S(2)}, u32[]{:S(2)}) collective-permute-start(bf16[4,32,16,128]{3,2,1,0:T(8,128)(2,1)S(1)} %slice_bitcast_fusion), channel_id=1, source_target_pairs={{0,1},{1,0},{2,3},{3,2},{4,5},{5,4},{6,7},{7,6},{8,9},{9,8},{10,11... | collective-permute-start | bytes 1572872 | tf_op jit(solution)/shard_map/ppermute | solution.py:421
  50.2 15.1 %collective-permute-start.12 = (f32[4,2,32,16]{3,2,1,0:T(8,128)S(1)}, f32[4,2,32,16]{3,2,1,0:T(8,128)S(1)}, u32[]{:S(2)}, u32[]{:S(2)}) collective-permute-start(f32[4,2,32,16]{3,2,1,0:T(8,128)S(1)} %slice_bitcast_fusion.5), channel_id=1, source_target_pairs={{0,1},{1,0},{2,3},{3,2},{4,5},{5,4},{6,7},{7,6},{8,9},{9,8},{10,11... | collective-permute-start | bytes 49160 | tf_op jit(solution)/shard_map/ppermute | solution.py:422
  50.7 44.8 %collective-permute-start.8 = (bf16[64,4096]{1,0:T(8,128)(2,1)}, bf16[64,4096]{1,0:T(8,128)(2,1)S(1)}, u32[]{:S(2)}, u32[]{:S(2)}) collective-permute-start(bf16[64,4096]{1,0:T(8,128)(2,1)} %collective-permute-done.7.refs_4_), channel_id=1, source_target_pairs={{0,1},{1,0},{2,3},{3,2},{4,5},{5,4},{6,7},{7,6},{8,9},{9,8},{10,11... | collective-permute-start | bytes 1572872 | tf_op jit(solution)/shard_map/ppermute | solution.py:418
  51.5 1.0 copy-start.2
  63.7 3.0 %copy-start.3 = (bf16[64,4096]{1,0:T(8,128)(2,1)S(1)}, bf16[64,4096]{1,0:T(8,128)(2,1)}, u32[]{:S(2)}) copy-start(bf16[64,4096]{1,0:T(8,128)(2,1)} %shard_map.80.refs_2_) | copy-start | bytes 1572868
  63.7 31.8 %collective-permute-start.13 = (bf16[2,128,1024]{2,1,0:T(8,128)(2,1)S(1)}, bf16[2,128,1024]{2,1,0:T(8,128)(2,1)S(1)}, u32[]{:S(2)}, u32[]{:S(2)}) collective-permute-start(bf16[2,128,1024]{2,1,0:T(8,128)(2,1)S(1)} %get-tuple-element.21.refs_4_), channel_id=1, source_target_pairs={{0,2},{2,0},{1,3},{3,1},{4,6},{6,4},{5,7},{7,5},{8,10},{10,8},{9,1... | collective-permute-start | bytes 1572872 | tf_op jit(solution)/shard_map/ppermute | solution.py:443
  65.2 55.2 %copy-start.6 = (bf16[64,4096]{1,0:T(8,128)(2,1)}, bf16[64,4096]{1,0:T(8,128)(2,1)S(1)}, u32[]{:S(2)}) copy-start(bf16[64,4096]{1,0:T(8,128)(2,1)S(1)} %collective-permute-done.9.refs_6_) | copy-start | bytes 1572868
  65.3 30.2 %collective-permute-start.10 = (bf16[64,4096]{1,0:T(8,128)(2,1)S(1)}, bf16[64,4096]{1,0:T(8,128)(2,1)S(1)}, u32[]{:S(2)}, u32[]{:S(2)}) collective-permute-start(bf16[64,4096]{1,0:T(8,128)(2,1)S(1)} %collective-permute-done.9.refs_6_), channel_id=1, source_target_pairs={{0,1},{1,0},{2,3},{3,2},{4,5},{5,4},{6,7},{7,6},{8,9},{9,8},{10,11... | collective-permute-start | bytes 1572872 | tf_op jit(solution)/shard_map/ppermute | solution.py:419
  81.6 38.9 %collective-permute-start.15 = (bf16[2,128,1536]{2,1,0:T(8,128)(2,1)S(1)}, bf16[2,128,1536]{2,1,0:T(8,128)(2,1)S(1)}, u32[]{:S(2)}, u32[]{:S(2)}) collective-permute-start(bf16[2,128,1536]{2,1,0:T(8,128)(2,1)S(1)} %get-tuple-element.24.refs_4_), channel_id=1, source_target_pairs={{0,2},{2,0},{1,3},{3,1},{4,6},{6,4},{5,7},{7,5},{8,10},{10,8},{9,1... | collective-permute-start | bytes 2359304 | tf_op jit(solution)/shard_map/ppermute | solution.py:443
  82.9 30.5 %collective-permute-start.18 = (bf16[34,16,128]{2,1,0:T(8,128)(2,1)S(1)}, bf16[34,16,128]{2,1,0:T(8,128)(2,1)S(1)}, u32[]{:S(2)}, u32[]{:S(2)}) collective-permute-start(bf16[34,16,128]{2,1,0:T(8,128)(2,1)S(1)} %get-tuple-element.39), channel_id=1, source_target_pairs={{0,12},{4,8},{8,4},{12,0},{1,13},{5,9},{9,5},{13,1},{2,14},{6,10},... | collective-permute-start | bytes 417800 | tf_op jit(solution)/shard_map/ppermute | solution.py:426
  95.5 25.0 %copy-start.8 = (bf16[64,4096]{1,0:T(8,128)(2,1)}, bf16[64,4096]{1,0:T(8,128)(2,1)S(1)}, u32[]{:S(2)}) copy-start(bf16[64,4096]{1,0:T(8,128)(2,1)S(1)} %collective-permute-done.8.refs_5_) | copy-start | bytes 1572868
  95.5 25.0 %copy-start.10 = (bf16[64,4096]{1,0:T(8,128)(2,1)}, bf16[64,4096]{1,0:T(8,128)(2,1)S(1)}, u32[]{:S(2)}) copy-start(bf16[64,4096]{1,0:T(8,128)(2,1)S(1)} %collective-permute-done.10.refs_7_) | copy-start | bytes 1572868
  95.5 13.6 %copy-start.14 = (bf16[2,128,1024]{2,1,0:T(8,128)(2,1)}, bf16[2,128,1024]{2,1,0:T(8,128)(2,1)S(1)}, u32[]{:S(2)}) copy-start(bf16[2,128,1024]{2,1,0:T(8,128)(2,1)S(1)} %collective-permute-done.13.refs_9_.near_ref) | copy-start | bytes 1572868
  109.2 29.6 %copy-start.12 = (bf16[2,256,1024]{2,1,0:T(8,128)(2,1)}, bf16[2,256,1024]{2,1,0:T(8,128)(2,1)S(1)}, u32[]{:S(2)}) copy-start(bf16[2,256,1024]{2,1,0:T(8,128)(2,1)S(1)} %get-tuple-element.26.held_ref.kept_ref) | copy-start | bytes 3145732
  109.2 32.3 %collective-permute-start.14 = (bf16[2,128,1024]{2,1,0:T(8,128)(2,1)}, bf16[2,128,1024]{2,1,0:T(8,128)(2,1)}, u32[]{:S(2)}, u32[]{:S(2)}) collective-permute-start(bf16[2,128,1024]{2,1,0:T(8,128)(2,1)} %get-tuple-element.27), channel_id=1, source_target_pairs={{0,2},{2,0},{1,3},{3,1},{4,6},{6,4},{5,7},{7,5},{8,10},{10,8},{9,1... | collective-permute-start | bytes 1572872 | tf_op jit(solution)/shard_map/ppermute | solution.py:454
  110.7 33.1 %collective-permute-start.20 = (bf16[2,128,1024]{2,1,0:T(8,128)(2,1)}, bf16[2,128,1024]{2,1,0:T(8,128)(2,1)}, u32[]{:S(2)}, u32[]{:S(2)}) collective-permute-start(bf16[2,128,1024]{2,1,0:T(8,128)(2,1)} %get-tuple-element.25.refs_8_), channel_id=1, source_target_pairs={{0,2},{2,0},{1,3},{3,1},{4,6},{6,4},{5,7},{7,5},{8,10},{10,8},{9,1... | collective-permute-start | bytes 1572872 | tf_op jit(solution)/shard_map/ppermute | solution.py:443
  111.3 8.9 %collective-permute-start.17 = (bf16[34,16,128]{2,1,0:T(8,128)(2,1)S(1)}, bf16[34,16,128]{2,1,0:T(8,128)(2,1)S(1)}, u32[]{:S(2)}, u32[]{:S(2)}) collective-permute-start(bf16[34,16,128]{2,1,0:T(8,128)(2,1)S(1)} %get-tuple-element.40), channel_id=1, source_target_pairs={{0,8},{4,12},{8,0},{12,4},{1,9},{5,13},{9,1},{13,5},{2,10},{6,14},... | collective-permute-start | bytes 417800 | tf_op jit(solution)/shard_map/ppermute | solution.py:426
  113.4 25.3 %copy-start.17 = (bf16[34,16,128]{2,1,0:T(8,128)(2,1)}, bf16[34,16,128]{2,1,0:T(8,128)(2,1)S(1)}, u32[]{:S(2)}) copy-start(bf16[34,16,128]{2,1,0:T(8,128)(2,1)S(1)} %collective-permute-done.18.refs_12_.refs_3_) | copy-start | bytes 417796
  113.4 7.0 %collective-permute-start.16 = (bf16[34,16,128]{2,1,0:T(8,128)(2,1)S(1)}, bf16[34,16,128]{2,1,0:T(8,128)(2,1)S(1)}, u32[]{:S(2)}, u32[]{:S(2)}) collective-permute-start(bf16[34,16,128]{2,1,0:T(8,128)(2,1)S(1)} %get-tuple-element.41), channel_id=1, source_target_pairs={{0,4},{4,0},{8,12},{12,8},{1,5},{5,1},{9,13},{13,9},{2,6},{6,2},{1... | collective-permute-start | bytes 417800 | tf_op jit(solution)/shard_map/ppermute | solution.py:426
  120.2 18.6 %copy-start.18 = (bf16[34,16,128]{2,1,0:T(8,128)(2,1)}, bf16[34,16,128]{2,1,0:T(8,128)(2,1)S(1)}, u32[]{:S(2)}) copy-start(bf16[34,16,128]{2,1,0:T(8,128)(2,1)S(1)} %collective-permute-done.17.refs_11_.refs_2_) | copy-start | bytes 417796
  120.4 18.4 %copy-start.19 = (bf16[34,16,128]{2,1,0:T(8,128)(2,1)}, bf16[34,16,128]{2,1,0:T(8,128)(2,1)S(1)}, u32[]{:S(2)}) copy-start(bf16[34,16,128]{2,1,0:T(8,128)(2,1)S(1)} %collective-permute-done.16.refs_10_.refs_1_) | copy-start | bytes 417796
  120.4 18.4 %copy-start.13 = (bf16[2,128,1536]{2,1,0:T(8,128)(2,1)}, bf16[2,128,1536]{2,1,0:T(8,128)(2,1)S(1)}, u32[]{:S(2)}) copy-start(bf16[2,128,1536]{2,1,0:T(8,128)(2,1)S(1)} %collective-permute-done.15.refs_9_.near_ref) | copy-start | bytes 2359300
  138.8 1.2 copy-start.15
  140.0 3.9 %copy-start.7 = (bf16[64,4096]{1,0:T(8,128)(2,1)S(1)}, bf16[64,4096]{1,0:T(8,128)(2,1)}, u32[]{:S(2)}) copy-start(bf16[64,4096]{1,0:T(8,128)(2,1)} %copy-done.6) | copy-start | bytes 1572868
  140.0 3.9 %copy-start.9 = (bf16[64,4096]{1,0:T(8,128)(2,1)S(1)}, bf16[64,4096]{1,0:T(8,128)(2,1)}, u32[]{:S(2)}) copy-start(bf16[64,4096]{1,0:T(8,128)(2,1)} %copy-done.8) | copy-start | bytes 1572868
  140.0 29.2 %collective-permute-start.19 = (bf16[2,128,1536]{2,1,0:T(8,128)(2,1)}, bf16[2,128,1536]{2,1,0:T(8,128)(2,1)}, u32[]{:S(2)}, u32[]{:S(2)}) collective-permute-start(bf16[2,128,1536]{2,1,0:T(8,128)(2,1)} %get-tuple-element.31), channel_id=1, source_target_pairs={{0,2},{2,0},{1,3},{3,1},{4,6},{6,4},{5,7},{7,5},{8,10},{10,8},{9,1... | collective-permute-start | bytes 2359304 | tf_op jit(solution)/shard_map/ppermute | solution.py:454
  143.9 1.0 copy-start.11
  144.9 0.7 copy-start.20
  145.6 15.2 %copy-start.22 = (bf16[2,32,1024]{2,1,0:T(8,128)(2,1)S(1)}, bf16[2,32,1024]{2,1,0:T(8,128)(2,1)}, u32[]{:S(2)}) copy-start(bf16[2,32,1024]{2,1,0:T(8,128)(2,1)} %param.9) | copy-start | bytes 393220
  159.2 1.0 copy-start.16
  160.2 12.8 %collective-permute-start.21 = (bf16[2,128,1024]{2,1,0:T(8,128)(2,1)}, bf16[2,128,1024]{2,1,0:T(8,128)(2,1)S(1)}, u32[]{:S(2)}, u32[]{:S(2)}) collective-permute-start(bf16[2,128,1024]{2,1,0:T(8,128)(2,1)} %get-tuple-element.36), channel_id=1, source_target_pairs={{0,2},{2,0},{1,3},{3,1},{4,6},{6,4},{5,7},{7,5},{8,10},{10,8},{9,1... | collective-permute-start | bytes 1572872 | tf_op jit(solution)/shard_map/ppermute | solution.py:454
  173.1 0.8 copy-start.21
